TPU v7x, 512 devices: a whole 4x8x8 slice. The times are simulated.
512 devices in a mesh: pipe: 64 (over z_hi, x, y), tensor: 8 (over z_lo, core).
Axes of the slice: x: 4, y: 8, z: 8 (z_hi: 2, z_lo: 4; z = z_hi * 4 + z_lo), core: 2. Of those that a mesh axis runs over, the one named last changes fastest.
Arguments:
- inputs_a: bfloat16 [64, 224, 7168], P('pipe', None, 'tensor'), may hold values from -110 to 110
- inputs_b: bfloat16 [64, 224, 7168], P('pipe', None, 'tensor'), may hold values from -110 to 110
- sent_a: bfloat16 [64, 224, 7168], P('pipe', None, 'tensor'), may hold values from -6 to 6
- sent_b: bfloat16 [64, 224, 7168], P('pipe', None, 'tensor'), may hold values from -6 to 6
- gain_pair: float32 [64, 2, 7168], P('pipe', None, 'tensor'), may hold values from 0.5 to 2, as said below
- latent_gain_pair: float32 [64, 2, 256], P('pipe'), may hold values from 0.5 to 2, as said below
- compress_pair: bfloat16 [64, 2, 256, 7168], P('pipe', None, None, 'tensor'), as said below
- expand_pair: bfloat16 [64, 2, 256, 7168], P('pipe', None, None, 'tensor'), as said below
Outputs:
- input_grad_a: bfloat16 [64, 224, 7168], P('pipe', None, 'tensor')
- input_grad_b: bfloat16 [64, 224, 7168], P('pipe', None, 'tensor')
- grad_compress: bfloat16 [64, 256, 7168], P('pipe', None, 'tensor')
- grad_expand: bfloat16 [64, 256, 7168], P('pipe', None, 'tensor')
Inputs may be any that keep to these rules, and one draw needn't show every extreme that they name: gain_pair[r, 1] equals gain_pair[63 - r, 0] for every rank r. latent_gain_pair[r, 1] equals latent_gain_pair[63 - r, 0] for every rank r. compress_pair[r, 1] equals compress_pair[63 - r, 0] for every rank r. expand_pair[r, 1] equals expand_pair[63 - r, 0] for every rank r.
All inputs are finite; a program needn't handle non-finite values.
Results may differ from a plain program's by a relative error of at most 0.0061.
Values may be sent and summed in bfloat16 or wider, within the bound.
No kernel may reach another device: no remote copies, remote signals or barrier semaphores. Data moves between devices by JAX's collectives and lax.ppermute only.
A program may use at most 64 MiB of HBM per device.

v0:
```python
import jax
import jax.numpy as jnp
from jax import lax
from jax.sharding import PartitionSpec as P

EPSILON = 1e-06


def shifted(block, axis, distance):
    devices = range(lax.axis_size(axis))
    route = [((i - distance) % len(devices), i) for i in devices]
    return lax.ppermute(block, axis, route)


def from_partner(value, axis, stride):
    return lax.ppermute(value, axis, [(i, i ^ 1 << stride) for i in range(lax.axis_size(axis))])


def contract_last(left, right):
    return lax.dot_general(
        left, right, (((1,), (1,)), ((), ())), preferred_element_type=jnp.float32
    )


def contract_first(left, right):
    return lax.dot_general(
        left, right, (((0,), (0,)), ((), ())), preferred_element_type=jnp.float32
    )


def squared_rows(inputs):
    values = inputs.astype(jnp.float32)
    return jnp.sum(values * values, -1, keepdims=True)


def compress_part(inputs, square_total, feature_count, gain_row, w_compress):
    values = inputs.astype(jnp.float32)
    rms_rows = jnp.sqrt(square_total / feature_count + EPSILON)
    unit_rows = values / rms_rows
    normed = (unit_rows * gain_row).astype(jnp.bfloat16)
    return (unit_rows, rms_rows, normed, contract_last(normed, w_compress))


def latent_backward(latent, grad_code, latent_gain, w_compress, unit_rows, gain_row):
    latent_rms = jnp.sqrt(jnp.mean(latent * latent, -1, keepdims=True) + EPSILON)
    latent_unit = latent / latent_rms
    latent_code = (latent_unit * latent_gain).astype(jnp.bfloat16)
    grad_unit = grad_code * latent_gain
    latent_centre = jnp.mean(grad_unit * latent_unit, -1, keepdims=True)
    grad_latent = ((grad_unit - latent_unit * latent_centre) / latent_rms).astype(jnp.bfloat16)
    grad_normed = jnp.dot(grad_latent, w_compress, preferred_element_type=jnp.float32)
    scaled = grad_normed * gain_row
    return (latent_code, grad_latent, scaled, jnp.sum(scaled * unit_rows, -1, keepdims=True))


def finish_input(cotangent, scaled, unit_rows, rms_rows, centre_total, feature_count):
    centre = centre_total / feature_count
    return (cotangent.astype(jnp.float32) + (scaled - unit_rows * centre) / rms_rows).astype(
        jnp.bfloat16
    )


def shards(
    inputs_a, inputs_b, sent_a, sent_b, gain_pair, latent_gain_pair, compress_pair, expand_pair
):
    arrive_a = shifted(sent_a, "pipe", -1)
    arrive_b = shifted(sent_b, "pipe", 1)
    local_a, local_b = (inputs_a[0], inputs_b[0])
    cot_a, cot_b = (arrive_a[0], arrive_b[0])
    feature_count = local_a.shape[1] * lax.axis_size("tensor")
    square_a, square_b, grad_code_a, grad_code_b = lax.psum(
        (
            squared_rows(local_a),
            squared_rows(local_b),
            contract_last(cot_a, expand_pair[0, 0]),
            contract_last(cot_b, expand_pair[0, 1]),
        ),
        "tensor",
    )
    unit_a, rms_a, normed_a, latent_part_a = compress_part(
        local_a, square_a, feature_count, gain_pair[0, 0], compress_pair[0, 0]
    )
    unit_b, rms_b, normed_b, latent_part_b = compress_part(
        local_b, square_b, feature_count, gain_pair[0, 1], compress_pair[0, 1]
    )
    latent_a, latent_b = lax.psum((latent_part_a, latent_part_b), "tensor")
    code_a, grad_latent_a, scaled_a, centre_part_a = latent_backward(
        latent_a, grad_code_a, latent_gain_pair[0, 0], compress_pair[0, 0], unit_a, gain_pair[0, 0]
    )
    code_b, grad_latent_b, scaled_b, centre_part_b = latent_backward(
        latent_b, grad_code_b, latent_gain_pair[0, 1], compress_pair[0, 1], unit_b, gain_pair[0, 1]
    )
    compress_b = contract_first(grad_latent_b, normed_b)
    expand_b = contract_first(code_b, cot_b)
    carried = jnp.concatenate([compress_b, expand_b], 0).astype(jnp.bfloat16)
    centre_a, centre_b = lax.psum((centre_part_a, centre_part_b), "tensor")
    grad_in_a = finish_input(cot_a, scaled_a, unit_a, rms_a, centre_a, feature_count)
    grad_in_b = finish_input(cot_b, scaled_b, unit_b, rms_b, centre_b, feature_count)
    compress_a = contract_first(grad_latent_a, normed_a)
    expand_a = contract_first(code_a, cot_a)
    levels = lax.axis_size("pipe").bit_length() - 1
    for bit_index in range(levels):
        carried = from_partner(carried, "pipe", bit_index)
    latent_units = compress_a.shape[0]
    received = carried.astype(jnp.float32)
    grad_compress = (compress_a + received[:latent_units]).astype(jnp.bfloat16)
    grad_expand = (expand_a + received[latent_units:]).astype(jnp.bfloat16)
    return (grad_in_a[None], grad_in_b[None], grad_compress[None], grad_expand[None])


def solution(mesh):
    placed = (
        P("pipe", None, "tensor"),
        P("pipe", None, "tensor"),
        P("pipe", None, "tensor"),
        P("pipe", None, "tensor"),
        P("pipe", None, "tensor"),
        P("pipe", None, None),
        P("pipe", None, None, "tensor"),
        P("pipe", None, None, "tensor"),
    )
    return jax.shard_map(
        shards,
        mesh=mesh,
        in_specs=placed,
        out_specs=(
            P("pipe", None, "tensor"),
            P("pipe", None, "tensor"),
            P("pipe", None, "tensor"),
            P("pipe", None, "tensor"),
        ),
        check_vma=False,
    )
```

profile of v0, /device:TPU:153, one launch (start us, length us, event | category | flops | bytes accessed | tf_op | source)
XLA Modules:
  0.0 351.0 jit_solution(1059130014680763993)
XLA Ops:
  7.2 0.0 all-reduce.5.cloned.1.call-start
  7.2 2.1 collective-permute-start
  9.3 4.4 %collective-permute-start.1 = (bf16[1,224,896]{2,1,0:T(8,128)(2,1)}, bf16[1,224,896]{2,1,0:T(8,128)(2,1)S(1)}, u32[]{:S(2)}, u32[]{:S(2)}) collective-permute-start(bf16[1,224,896]{2,1,0:T(8,128)(2,1)} %param.11), channel_id=1, source_target_pairs={{504,0},{0,8},{8,16},{16,24},{24,32},{32,40},{40,48},{48,56},{56,6... | collective-permute-start | bytes 1204232 | tf_op jit(solution)/shard_map/ppermute | solution.py:12
  13.7 1.2 fusion.6
  14.9 1.2 fusion.9
  16.0 0.8 slice_reduce_fusion
  16.8 11.4 %all-reduce.1 = (f32[224,1]{0,1:T(1,128)S(1)}, f32[224,1]{0,1:T(1,128)S(1)}) all-reduce(f32[224,1]{0,1:T(1,128)S(1)} %bitcast.97, f32[224,1]{0,1:T(1,128)S(1)} %bitcast.98), channel_id=1, replica_groups=mesh['pipe'=64,'tensor'=8] {'tensor'}, use_global_device_ids=true, to_apply=%region_2.0 | all-reduce | flops 448 | bytes 3584 | tf_op jit(solution)/shard_map/psum | solution.py:71
  28.2 0.0 copy-start.2
  28.2 0.0 copy-start.9
  28.2 2.3 fusion.15
  30.5 0.0 copy-done.2
  30.5 1.0 fusion.20
  31.6 0.0 collective-permute-done
  31.6 0.1 copy-done.4
  31.7 1.0 fusion.22
  32.7 0.0 collective-permute-done.1
  32.7 1.0 fusion.17
  33.7 0.0 all-reduce.5.cloned.1.call-update
  33.8 0.0 copy-done.8
  33.8 94.0 %all-reduce.5.cloned.1.call-done = (f32[224,256]{1,0:T(8,128)}, f32[224,256]{1,0:T(8,128)}, f32[224,256]{1,0:T(8,128)}, f32[224,256]{1,0:T(8,128)}) async-done(((f32[224,256]{1,0:T(8,128)}, f32[224,256]{1,0:T(8,128)}, f32[224,256]{1,0:T(8,128)}, f32[224,256]{1,0:T(8,128)}), (f32[224,256]{1,0:T(8,128)}, f32[224,256]{1,0:T(8,128)}, f32[224,256]{1,0:T(8,128)}, ...) | async-done | bytes 917520 | tf_op jit(solution)/shard_map/psum | solution.py:71
  127.8 1.0 multiply_reduce_fusion.3
  128.9 1.2 multiply_reduce_fusion.2
  130.2 1.6 convolution_convert_fusion.1
  131.8 0.0 copy-start.10
  131.8 0.4 convolution_convert_fusion
  132.2 0.1 pad_maximum_fusion
  132.3 2.3 collective-permute-start.2
  134.6 21.7 %collective-permute-done.2 = bf16[512,896]{1,0:T(8,128)(2,1)S(1)} collective-permute-done((bf16[512,896]{1,0:T(8,128)(2,1)S(1)}, bf16[512,896]{1,0:T(8,128)(2,1)S(1)}, u32[]{:S(2)}, u32[]{:S(2)}) %collective-permute-start.2) | collective-permute-done | bytes 917536 | tf_op jit(solution)/shard_map/ppermute | solution.py:16
  156.3 2.1 collective-permute-start.3
  158.4 42.5 %collective-permute-done.3 = bf16[512,896]{1,0:T(8,128)(2,1)S(1)} collective-permute-done((bf16[512,896]{1,0:T(8,128)(2,1)S(1)}, bf16[512,896]{1,0:T(8,128)(2,1)S(1)}, u32[]{:S(2)}, u32[]{:S(2)}) %collective-permute-start.3) | collective-permute-done | bytes 917536 | tf_op jit(solution)/shard_map/ppermute | solution.py:16
  201.0 3.5 %collective-permute-start.4 = (bf16[512,896]{1,0:T(8,128)(2,1)S(1)}, bf16[512,896]{1,0:T(8,128)(2,1)S(1)}, u32[]{:S(2)}, u32[]{:S(2)}) collective-permute-start(bf16[512,896]{1,0:T(8,128)(2,1)S(1)} %collective-permute-done.3), channel_id=1, source_target_pairs={{0,32},{8,40},{16,48},{24,56},{32,0},{40,8},{48,16},{56,24},{64,96... | collective-permute-start | bytes 2752520 | tf_op jit(solution)/shard_map/ppermute | solution.py:16
  204.5 42.7 %collective-permute-done.4 = bf16[512,896]{1,0:T(8,128)(2,1)S(1)} collective-permute-done((bf16[512,896]{1,0:T(8,128)(2,1)S(1)}, bf16[512,896]{1,0:T(8,128)(2,1)S(1)}, u32[]{:S(2)}, u32[]{:S(2)}) %collective-permute-start.4) | collective-permute-done | bytes 917536 | tf_op jit(solution)/shard_map/ppermute | solution.py:16
  247.3 3.0 collective-permute-start.5
  250.3 0.1 multiply_reduce_fusion.5
  250.4 20.2 %collective-permute-done.5 = bf16[512,896]{1,0:T(8,128)(2,1)} collective-permute-done((bf16[512,896]{1,0:T(8,128)(2,1)S(1)}, bf16[512,896]{1,0:T(8,128)(2,1)}, u32[]{:S(2)}, u32[]{:S(2)}) %collective-permute-start.5) | collective-permute-done | bytes 917536 | tf_op jit(solution)/shard_map/ppermute | solution.py:16
  270.6 4.6 %collective-permute-start.6 = (bf16[512,896]{1,0:T(8,128)(2,1)}, bf16[512,896]{1,0:T(8,128)(2,1)}, u32[]{:S(2)}, u32[]{:S(2)}) collective-permute-start(bf16[512,896]{1,0:T(8,128)(2,1)} %collective-permute-done.5), channel_id=1, source_target_pairs={{0,128},{8,136},{16,144},{24,152},{32,160},{40,168},{48,176},{56,1... | collective-permute-start | bytes 2752520 | tf_op jit(solution)/shard_map/ppermute | solution.py:16
  275.2 0.2 multiply_reduce_fusion.4
  275.4 0.4 multiply_reduce_fusion
  275.9 0.4 multiply_reduce_fusion.1
  276.3 13.8 %all-reduce = (f32[224,1]{0,1:T(1,128)S(1)}, f32[224,1]{0,1:T(1,128)S(1)}) all-reduce(f32[224,1]{0,1:T(1,128)S(1)} %bitcast.113, f32[224,1]{0,1:T(1,128)S(1)} %bitcast.112), channel_id=1, replica_groups=mesh['pipe'=64,'tensor'=8] {'tensor'}, use_global_device_ids=true, to_apply=%region_7.0 | all-reduce | flops 448 | bytes 3584 | tf_op jit(solution)/shard_map/psum | solution.py:96
  290.1 4.7 %collective-permute-done.6 = bf16[512,896]{1,0:T(8,128)(2,1)} collective-permute-done((bf16[512,896]{1,0:T(8,128)(2,1)}, bf16[512,896]{1,0:T(8,128)(2,1)}, u32[]{:S(2)}, u32[]{:S(2)}) %collective-permute-start.6) | collective-permute-done | bytes 917536 | tf_op jit(solution)/shard_map/ppermute | solution.py:16
  294.8 6.0 %collective-permute-start.7 = (bf16[512,896]{1,0:T(8,128)(2,1)}, bf16[512,896]{1,0:T(8,128)(2,1)S(1)}, u32[]{:S(2)}, u32[]{:S(2)}) collective-permute-start(bf16[512,896]{1,0:T(8,128)(2,1)} %collective-permute-done.6), channel_id=1, source_target_pairs={{0,256},{8,264},{16,272},{24,280},{32,288},{40,296},{48,304},{56,3... | collective-permute-start | bytes 2752520 | tf_op jit(solution)/shard_map/ppermute | solution.py:16
  300.9 1.0 fusion.48
  301.9 1.0 fusion.49
  302.9 38.6 %collective-permute-done.7 = bf16[512,896]{1,0:T(8,128)(2,1)S(1)} collective-permute-done((bf16[512,896]{1,0:T(8,128)(2,1)}, bf16[512,896]{1,0:T(8,128)(2,1)S(1)}, u32[]{:S(2)}, u32[]{:S(2)}) %collective-permute-start.7) | collective-permute-done | bytes 917536 | tf_op jit(solution)/shard_map/ppermute | solution.py:16
  341.6 0.1 convert_element_type.89
  341.7 1.2 fusion.12
  343.0 1.2 fusion.13
  (24 shorter events, 0.1 us)
Async XLA Ops:
  7.2 120.6 %all-reduce.5.cloned.1.call-start = ((), (), s32[]{:S(2)}) async-start(), calls=%async_computation | async-start | bytes 1835008 | tf_op jit(solution)/shard_map/psum | solution.py:71
  7.2 24.4 %collective-permute-start = (bf16[1,224,896]{2,1,0:T(8,128)(2,1)}, bf16[1,224,896]{2,1,0:T(8,128)(2,1)S(1)}, u32[]{:S(2)}, u32[]{:S(2)}) collective-permute-start(bf16[1,224,896]{2,1,0:T(8,128)(2,1)} %param.10), channel_id=1, source_target_pairs={{8,0},{16,8},{24,16},{32,24},{40,32},{48,40},{56,48},{64,56},{72,6... | collective-permute-start | bytes 1204232 | tf_op jit(solution)/shard_map/ppermute | solution.py:12
  9.3 23.4 %collective-permute-start.1 = (bf16[1,224,896]{2,1,0:T(8,128)(2,1)}, bf16[1,224,896]{2,1,0:T(8,128)(2,1)S(1)}, u32[]{:S(2)}, u32[]{:S(2)}) collective-permute-start(bf16[1,224,896]{2,1,0:T(8,128)(2,1)} %param.11), channel_id=1, source_target_pairs={{504,0},{0,8},{8,16},{16,24},{24,32},{32,40},{40,48},{48,56},{56,6... | collective-permute-start | bytes 1204232 | tf_op jit(solution)/shard_map/ppermute | solution.py:12
  28.2 2.3 copy-start.2
  28.2 2.3 copy-start.9
  30.5 1.2 copy-start.4
  31.6 2.2 copy-start.8
  31.6 98.6 %copy-start.1 = (bf16[1,224,896]{2,1,0:T(8,128)(2,1)S(1)}, bf16[1,224,896]{2,1,0:T(8,128)(2,1)}, u32[]{:S(2)}) copy-start(bf16[1,224,896]{2,1,0:T(8,128)(2,1)} %param.9) | copy-start | bytes 1204228
  130.1 1.6 copy-start.3
  131.7 118.6 %copy-start = (f32[224,256]{1,0:T(8,128)S(1)}, f32[224,256]{1,0:T(8,128)}, u32[]{:S(2)}) copy-start(f32[224,256]{1,0:T(8,128)} %get-tuple-element.11) | copy-start | bytes 688132
  131.7 143.5 %copy-start.5 = (f32[224,256]{1,0:T(8,128)S(1)}, f32[224,256]{1,0:T(8,128)}, u32[]{:S(2)}) copy-start(f32[224,256]{1,0:T(8,128)} %get-tuple-element.10) | copy-start | bytes 688132
  131.7 143.7 %copy-start.7 = (f32[224,256]{1,0:T(8,128)S(1)}, f32[224,256]{1,0:T(8,128)}, u32[]{:S(2)}) copy-start(f32[224,256]{1,0:T(8,128)} %get-tuple-element.12) | copy-start | bytes 688132
  131.8 143.7 %copy-start.10 = (bf16[1,2,256,896]{3,2,1,0:T(8,128)(2,1)S(1)}, bf16[1,2,256,896]{3,2,1,0:T(8,128)(2,1)}, u32[]{:S(2)}) copy-start(bf16[1,2,256,896]{3,2,1,0:T(8,128)(2,1)} %param.14) | copy-start | bytes 2752516
  132.3 24.0 %collective-permute-start.2 = (bf16[512,896]{1,0:T(8,128)(2,1)S(1)}, bf16[512,896]{1,0:T(8,128)(2,1)S(1)}, u32[]{:S(2)}, u32[]{:S(2)}) collective-permute-start(bf16[512,896]{1,0:T(8,128)(2,1)S(1)} %pad_maximum_fusion), channel_id=1, source_target_pairs={{0,8},{8,0},{16,24},{24,16},{32,40},{40,32},{48,56},{56,48},{64,72... | collective-permute-start | bytes 2752520 | tf_op jit(solution)/shard_map/ppermute | solution.py:16
  156.3 44.7 %collective-permute-start.3 = (bf16[512,896]{1,0:T(8,128)(2,1)S(1)}, bf16[512,896]{1,0:T(8,128)(2,1)S(1)}, u32[]{:S(2)}, u32[]{:S(2)}) collective-permute-start(bf16[512,896]{1,0:T(8,128)(2,1)S(1)} %collective-permute-done.2), channel_id=1, source_target_pairs={{0,16},{8,24},{16,0},{24,8},{32,48},{40,56},{48,32},{56,40},{64,80... | collective-permute-start | bytes 2752520 | tf_op jit(solution)/shard_map/ppermute | solution.py:16
  201.0 46.3 %collective-permute-start.4 = (bf16[512,896]{1,0:T(8,128)(2,1)S(1)}, bf16[512,896]{1,0:T(8,128)(2,1)S(1)}, u32[]{:S(2)}, u32[]{:S(2)}) collective-permute-start(bf16[512,896]{1,0:T(8,128)(2,1)S(1)} %collective-permute-done.3), channel_id=1, source_target_pairs={{0,32},{8,40},{16,48},{24,56},{32,0},{40,8},{48,16},{56,24},{64,96... | collective-permute-start | bytes 2752520 | tf_op jit(solution)/shard_map/ppermute | solution.py:16
  247.3 23.4 %collective-permute-start.5 = (bf16[512,896]{1,0:T(8,128)(2,1)S(1)}, bf16[512,896]{1,0:T(8,128)(2,1)}, u32[]{:S(2)}, u32[]{:S(2)}) collective-permute-start(bf16[512,896]{1,0:T(8,128)(2,1)S(1)} %collective-permute-done.4), channel_id=1, source_target_pairs={{0,64},{8,72},{16,80},{24,88},{32,96},{40,104},{48,112},{56,120},{... | collective-permute-start | bytes 2752520 | tf_op jit(solution)/shard_map/ppermute | solution.py:16
  270.6 24.2 %collective-permute-start.6 = (bf16[512,896]{1,0:T(8,128)(2,1)}, bf16[512,896]{1,0:T(8,128)(2,1)}, u32[]{:S(2)}, u32[]{:S(2)}) collective-permute-start(bf16[512,896]{1,0:T(8,128)(2,1)} %collective-permute-done.5), channel_id=1, source_target_pairs={{0,128},{8,136},{16,144},{24,152},{32,160},{40,168},{48,176},{56,1... | collective-permute-start | bytes 2752520 | tf_op jit(solution)/shard_map/ppermute | solution.py:16
  294.8 46.8 %collective-permute-start.7 = (bf16[512,896]{1,0:T(8,128)(2,1)}, bf16[512,896]{1,0:T(8,128)(2,1)S(1)}, u32[]{:S(2)}, u32[]{:S(2)}) collective-permute-start(bf16[512,896]{1,0:T(8,128)(2,1)} %collective-permute-done.6), channel_id=1, source_target_pairs={{0,256},{8,264},{16,272},{24,280},{32,288},{40,296},{48,304},{56,3... | collective-permute-start | bytes 2752520 | tf_op jit(solution)/shard_map/ppermute | solution.py:16
  302.9 38.8 %copy-start.6 = (f32[224,256]{1,0:T(8,128)S(1)}, f32[224,256]{1,0:T(8,128)}, u32[]{:S(2)}) copy-start(f32[224,256]{1,0:T(8,128)} %get-tuple-element.10) | copy-start | bytes 688132
Sparse Core Ops, SparseCore 0:
  33.9 93.8 all-reduce.4
where the time goes:
time: 352 us; the launch traced here: 351 us
  waiting for transfers between devices  265 us (75%)
  starting transfers between devices  28.1 us (8%)
  blocking collectives  25.2 us (7%)
  between operations  14.3 us (4%)
  matrix products  10.6 us (3%)
  other arithmetic  7.23 us (2%)
    ppermute x6, waiting for transfers between devices, from_partner(): lax.ppermute(value, axis, [(i, i ^ 1 << stride) for i in range(lax.axis_s...  171 us
    psum x1, waiting for transfers between devices, shards(): lax.psum((squared_rows(local_a), squared_rows(local_b), contract_last(cot...  94 us
    ppermute x6, starting transfers between devices, from_partner(): lax.ppermute(value, axis, [(i, i ^ 1 << stride) for i in range(lax.axis_s...  21.6 us
    psum x1, blocking collectives, shards(): centre_a, centre_b = lax.psum((centre_part_a, centre_part_b), 'tensor')  13.8 us
    psum x1, blocking collectives, shards(): lax.psum((squared_rows(local_a), squared_rows(local_b), contract_last(cot...  11.4 us
  transfers between devices with their start and end apart: 9, of which 7 were waited for; matrix products, arithmetic and copies ran while one was open for 3% of the time, Pallas kernels for 0%

commit v1 on v0

v1 whole, which is shorter than its diff:
```python
import jax
import jax.numpy as jnp
from jax import lax
from jax.experimental import pallas as pl
from jax.experimental.pallas import tpu as pltpu
from jax.sharding import PartitionSpec as P

EPSILON = 1e-06
TOKENS = 224
PADDED = 256
HALF = 128
PART = 32
WIDTH = 896
UNITS = 256
FEATURES = 7168
SUM_COLS = 4 * UNITS + 128
OWN_COLS = 3 * UNITS + 128
MIR_COLS = 2 * UNITS
ALL_COLS = OWN_COLS + MIR_COLS
F32 = jnp.float32
BF16 = jnp.bfloat16


def contract_last(left, right):
    return lax.dot_general(left, right, (((1,), (1,)), ((), ())), preferred_element_type=F32)


def contract_first(left, right):
    return lax.dot_general(left, right, (((0,), (0,)), ((), ())), preferred_element_type=F32)


def lanes(rows):
    return lax.broadcasted_iota(jnp.int32, (rows, 128), 1)


def split_pair(first, second):
    lane = lanes(first.shape[0])
    value = jnp.where(lane % 2 == 0, first, second)
    high = value.astype(BF16).astype(F32)
    packed = jnp.where(lane < 2, high, value - high)
    return jnp.where(lane < 4, packed, 0.0).astype(BF16)


def joined(block):
    block = block.astype(F32)
    return block[:, 0:1] + block[:, 2:3], block[:, 1:2] + block[:, 3:4]


def latent_kernel(xa_ref, xb_ref, gain_ref, wc_ref, xga_ref, xgb_ref, lat_ref):
    squares = []
    for s, (x_ref, xg_ref) in enumerate(((xa_ref, xga_ref), (xb_ref, xgb_ref))):
        x = x_ref[0].astype(F32)
        xg = (x * gain_ref[0, s : s + 1, :]).astype(BF16)
        xg_ref[...] = xg
        lat_ref[0:TOKENS, s * UNITS : (s + 1) * UNITS] = contract_last(xg, wc_ref[0, s])
        squares.append(jnp.sum(x * x, -1, keepdims=True))
    lane = lanes(TOKENS)
    block = jnp.where(lane == 0, squares[0], jnp.where(lane == 1, squares[1], 0.0))
    lat_ref[0:TOKENS, 2 * UNITS :] = block
    lat_ref[TOKENS:, :] = jnp.zeros((PADDED - TOKENS, 2 * UNITS + 128), F32)


def code_kernel(ca_ref, cb_ref, we_ref, lat_ref, keep_ref, send_ref, full):
    for s, c_ref in enumerate((ca_ref, cb_ref)):
        full[0:TOKENS, s * UNITS : (s + 1) * UNITS] = contract_last(c_ref[0], we_ref[0, s])
    full[TOKENS:, :] = jnp.zeros((PADDED - TOKENS, 2 * UNITS), F32)
    core = lax.rem(lax.axis_index("tensor"), 2)
    mine = pl.ds(pl.multiple_of(core * HALF, HALF), HALF)
    other = pl.ds(pl.multiple_of((1 - core) * HALF, HALF), HALF)
    keep_ref[:, 0 : 2 * UNITS] = lat_ref[mine, 0 : 2 * UNITS]
    keep_ref[:, 2 * UNITS : 4 * UNITS] = full[mine, :]
    keep_ref[:, 4 * UNITS :] = lat_ref[mine, 2 * UNITS :]
    send_ref[:, 0 : 2 * UNITS] = lat_ref[other, 0 : 2 * UNITS].astype(BF16)
    send_ref[:, 2 * UNITS : 4 * UNITS] = full[other, :].astype(BF16)
    block = lat_ref[other, 2 * UNITS :]
    send_ref[:, 4 * UNITS :] = split_pair(block[:, 0:1], block[:, 1:2])


def scatter_kernel(keep_ref, recv_ref, own_ref, one_ref, two_ref, three_ref, total):
    total[...] = keep_ref[...] + recv_ref[...].astype(F32)
    spot = lax.div(lax.axis_index("tensor"), 2)

    def rows(d):
        return pl.ds(pl.multiple_of((spot ^ d) * PART, PART), PART)

    own_ref[...] = total[rows(0), :]
    for d, ref in ((1, one_ref), (2, two_ref), (3, three_ref)):
        ref[:, 0 : 4 * UNITS] = total[rows(d), 0 : 4 * UNITS].astype(BF16)
        ref[:, 4 * UNITS :] = split_pair(*joined(total[rows(d), 4 * UNITS :]))


def latent_backward(latent_sum, grad_code, square, latent_gain):
    rms = jnp.sqrt(square / FEATURES + EPSILON)
    latent = latent_sum / rms
    latent_rms = jnp.sqrt(jnp.mean(latent * latent, -1, keepdims=True) + EPSILON)
    latent_unit = latent / latent_rms
    code = (latent_unit * latent_gain).astype(BF16)
    grad_unit = grad_code * latent_gain
    latent_centre = jnp.mean(grad_unit * latent_unit, -1, keepdims=True)
    grad_latent = (grad_unit - latent_unit * latent_centre) / latent_rms
    ratio = (grad_latent / rms).astype(BF16)
    centre = jnp.sum(ratio.astype(F32) * latent, -1, keepdims=True) / FEATURES / rms
    return ratio, code, centre


def latent_step_kernel(own_ref, one_ref, two_ref, three_ref, gain_ref, out_ref, mir_ref):
    total = own_ref[...]
    for ref in (one_ref, two_ref, three_ref):
        total = total + ref[...].astype(F32)
    square_a, square_b = joined(total[:, 4 * UNITS :])
    ratio_a, code_a, centre_a = latent_backward(
        total[:, 0:UNITS], total[:, 2 * UNITS : 3 * UNITS], square_a, gain_ref[0, 0:1, :]
    )
    ratio_b, code_b, centre_b = latent_backward(
        total[:, UNITS : 2 * UNITS], total[:, 3 * UNITS : 4 * UNITS], square_b, gain_ref[0, 1:2, :]
    )
    out_ref[:, 0:UNITS] = ratio_a
    out_ref[:, UNITS : 2 * UNITS] = code_a
    out_ref[:, 2 * UNITS : 3 * UNITS] = ratio_b
    out_ref[:, 3 * UNITS :] = split_pair(centre_a, centre_b)
    mir_ref[:, 0:UNITS] = ratio_b
    mir_ref[:, UNITS:] = code_b


def gather_kernel(own_ref, one_ref, two_ref, three_ref, out_ref):
    spot = lax.div(lax.axis_index("tensor"), 2)
    for d, ref in enumerate((own_ref, one_ref, two_ref, three_ref)):
        out_ref[pl.ds(pl.multiple_of((spot ^ d) * PART, PART), PART), :] = ref[...]


def finish_kernel(
    mine_ref, other_ref, ca_ref, cb_ref, xa_ref, xb_ref, xga_ref, xm_ref, cm_ref, gain_ref, wc_ref,
    ia_ref, ib_ref, gc_ref, ge_ref, full,
):
    core = lax.rem(lax.axis_index("tensor"), 2)
    full[pl.ds(pl.multiple_of(core * HALF, HALF), HALF), :] = mine_ref[...]
    full[pl.ds(pl.multiple_of((1 - core) * HALF, HALF), HALF), :] = other_ref[...]
    ratio_a = full[0:TOKENS, 0:UNITS]
    code_a = full[0:TOKENS, UNITS : 2 * UNITS]
    ratio_b = full[0:TOKENS, 2 * UNITS : 3 * UNITS]
    centres = joined(full[0:TOKENS, 3 * UNITS : OWN_COLS])
    ratio_m = full[0:TOKENS, OWN_COLS : OWN_COLS + UNITS]
    code_m = full[0:TOKENS, OWN_COLS + UNITS :]
    streams = ((ratio_a, ca_ref, xa_ref, ia_ref), (ratio_b, cb_ref, xb_ref, ib_ref))
    for s, (ratio, c_ref, x_ref, i_ref) in enumerate(streams):
        grad = jnp.dot(ratio, wc_ref[0, s], preferred_element_type=F32) * gain_ref[0, s : s + 1, :]
        i_ref[0] = (
            c_ref[0].astype(F32) + (grad - x_ref[0].astype(F32) * centres[s])
        ).astype(BF16)
    xg_m = (xm_ref[0].astype(F32) * gain_ref[0, 0:1, :]).astype(BF16)
    mirror = contract_first(ratio_m, xg_m).astype(BF16).astype(F32)
    gc_ref[0] = (contract_first(ratio_a, xga_ref[...]) + mirror).astype(BF16)
    mirror = contract_first(code_m, cm_ref[0]).astype(BF16).astype(F32)
    ge_ref[0] = (contract_first(code_a, ca_ref[0]) + mirror).astype(BF16)


def call(kernel, outs, scratch=(), flops=0, name=None):
    return pl.pallas_call(
        kernel,
        out_shape=[jax.ShapeDtypeStruct(shape, dtype) for shape, dtype in outs],
        scratch_shapes=[pltpu.VMEM(shape, dtype) for shape, dtype in scratch],
        compiler_params=pltpu.CompilerParams(vmem_limit_bytes=40 * 2**20),
        cost_estimate=pl.CostEstimate(flops=flops, bytes_accessed=4 * 2**20, transcendentals=0),
        name=name,
    )


def shards(xa, xb, sent_a, sent_b, gain, latent_gain, wc, we):
    pipe = range(lax.axis_size("pipe"))
    last = len(pipe) - 1
    tensor = range(lax.axis_size("tensor"))

    def swap(value, d):
        return lax.ppermute(value, "tensor", [(i, i ^ d) for i in tensor])

    ca = lax.ppermute(sent_a, "pipe", [((i + 1) % len(pipe), i) for i in pipe])
    cb = lax.ppermute(sent_b, "pipe", [(i, (i + 1) % len(pipe)) for i in pipe])
    xm = lax.ppermute(xb, "pipe", [(i, last - i) for i in pipe])
    cm = lax.ppermute(sent_b, "pipe", [(i, (last - 1 - i) % len(pipe)) for i in pipe])

    xga, xgb, lat = call(
        latent_kernel,
        [((TOKENS, WIDTH), BF16), ((TOKENS, WIDTH), BF16), ((PADDED, 2 * UNITS + 128), F32)],
        flops=2 * 2 * TOKENS * WIDTH * UNITS,
        name="latent",
    )(xa, xb, gain, wc)
    keep, send = call(
        code_kernel,
        [((HALF, SUM_COLS), F32), ((HALF, SUM_COLS), BF16)],
        [((PADDED, 2 * UNITS), F32)],
        flops=2 * 2 * TOKENS * WIDTH * UNITS,
        name="code",
    )(ca, cb, we, lat)
    own, *parts = call(
        scatter_kernel,
        [((PART, SUM_COLS), F32)] + [((PART, SUM_COLS), BF16)] * 3,
        [((HALF, SUM_COLS), F32)],
        name="scatter",
    )(keep, swap(send, 1))
    parts = [swap(part, 2 * d) for d, part in zip((1, 2, 3), parts)]
    out, mir = call(
        latent_step_kernel,
        [((PART, OWN_COLS), BF16), ((PART, MIR_COLS), BF16)],
        name="step",
    )(own, *parts, latent_gain)
    mir = lax.ppermute(mir, "pipe", [(i, last - i) for i in pipe])
    out = jnp.concatenate([out, mir], 1)
    (mine,) = call(gather_kernel, [((HALF, ALL_COLS), BF16)], name="gather")(
        out, *(swap(out, 2 * d) for d in (1, 2, 3))
    )
    other = swap(mine, 1)
    big = ((1, TOKENS, WIDTH), BF16)
    grad = ((1, UNITS, WIDTH), BF16)
    return tuple(
        call(
            finish_kernel,
            [big, big, grad, grad],
            [((PADDED, ALL_COLS), BF16)],
            flops=6 * 2 * TOKENS * WIDTH * UNITS,
            name="finish",
        )(mine, other, ca, cb, xa, xb, xga, xm, cm, gain, wc)
    )


def solution(mesh):
    wide = P("pipe", None, "tensor")
    weights = P("pipe", None, None, "tensor")
    return jax.shard_map(
        shards,
        mesh=mesh,
        in_specs=(wide,) * 5 + (P("pipe", None, None), weights, weights),
        out_specs=(wide,) * 4,
        check_vma=False,
    )
```

time: 352 us -> 143 us (0.41)
  the two profiles are of different devices: /device:TPU:153 before, /device:TPU:1 now
where the time goes in v1:
time: 143 us; the launch traced here: 142 us
  waiting for transfers between devices  81.6 us (57%)
  starting transfers between devices  50.8 us (36%)
  Pallas kernels  4.77 us (3%)
  local copies, waits for them, and re-layouts  3.9 us (3%)
    ppermute x8, waiting for transfers between devices, swap(): return lax.ppermute(value, 'tensor', [(i, i ^ d) for i in tensor])  39.4 us
    ppermute x8, starting transfers between devices, swap(): return lax.ppermute(value, 'tensor', [(i, i ^ d) for i in tensor])  26.4 us
    ppermute x1, starting transfers between devices, shards(): ca = lax.ppermute(sent_a, 'pipe', [((i + 1) % len(pipe), i) for i in pipe])  16.6 us
    ppermute x1, waiting for transfers between devices, shards(): cb = lax.ppermute(sent_b, 'pipe', [(i, (i + 1) % len(pipe)) for i in pipe])  15.4 us
    ppermute x1, waiting for transfers between devices, shards(): mir = lax.ppermute(mir, 'pipe', [(i, last - i) for i in pipe])  11.1 us
    ppermute x1, waiting for transfers between devices, shards(): xm = lax.ppermute(xb, 'pipe', [(i, last - i) for i in pipe])  9.45 us
    ppermute x1, waiting for transfers between devices, shards(): ca = lax.ppermute(sent_a, 'pipe', [((i + 1) % len(pipe), i) for i in pipe])  6.29 us
    unnamed x23, local copies, waits for them, and re-layouts  3.9 us
  transfers between devices with their start and end apart: 13, of which 8 were waited for; matrix products, arithmetic and copies ran while one was open for 0% of the time, Pallas kernels for 1%

profile of v1, /device:TPU:1, one launch (start us, length us, event | category | flops | bytes accessed | tf_op | source)
XLA Modules:
  0.0 141.9 jit_solution(14086097499792786345)
XLA Ops:
  0.6 16.6 %collective-permute-start = (bf16[1,224,896]{2,1,0:T(8,128)(2,1)}, bf16[1,224,896]{2,1,0:T(8,128)(2,1)S(1)}, u32[]{:S(2)}, u32[]{:S(2)}) collective-permute-start(bf16[1,224,896]{2,1,0:T(8,128)(2,1)} %param.10), channel_id=1, source_target_pairs={{8,0},{16,8},{24,16},{32,24},{40,32},{48,40},{56,48},{64,56},{72,6... | collective-permute-start | bytes 1204232 | tf_op jit(solution)/shard_map/ppermute | solution.py:176
  17.2 1.9 %collective-permute-start.1 = (bf16[1,224,896]{2,1,0:T(8,128)(2,1)}, bf16[1,224,896]{2,1,0:T(8,128)(2,1)S(1)}, u32[]{:S(2)}, u32[]{:S(2)}) collective-permute-start(bf16[1,224,896]{2,1,0:T(8,128)(2,1)} %param.11), channel_id=1, source_target_pairs={{0,8},{8,16},{16,24},{24,32},{32,40},{40,48},{48,56},{56,64},{64,7... | collective-permute-start | bytes 1204232 | tf_op jit(solution)/shard_map/ppermute | solution.py:177
  19.1 0.0 copy-start
  19.1 1.2 copy-done
  20.3 0.0 copy-start.2
  20.3 1.0 copy-done.2
  21.3 0.0 copy-start.4
  21.3 1.0 copy-done.4
  22.3 0.0 copy-start.7
  22.3 0.7 copy-done.7
  23.0 1.2 latent.1
  24.2 6.3 %collective-permute-done.ca_ref = bf16[1,224,896]{2,1,0:T(8,128)(2,1)S(1)} collective-permute-done((bf16[1,224,896]{2,1,0:T(8,128)(2,1)}, bf16[1,224,896]{2,1,0:T(8,128)(2,1)S(1)}, u32[]{:S(2)}, u32[]{:S(2)}) %collective-permute-start) | collective-permute-done | bytes 401440 | tf_op jit(solution)/shard_map/ppermute | solution.py:176
  30.5 15.4 %collective-permute-done.1.cb_ref = bf16[1,224,896]{2,1,0:T(8,128)(2,1)S(1)} collective-permute-done((bf16[1,224,896]{2,1,0:T(8,128)(2,1)}, bf16[1,224,896]{2,1,0:T(8,128)(2,1)S(1)}, u32[]{:S(2)}, u32[]{:S(2)}) %collective-permute-start.1) | collective-permute-done | bytes 401440 | tf_op jit(solution)/shard_map/ppermute | solution.py:177
  45.8 0.0 copy-done.6
  45.8 0.5 code.1
  46.4 5.2 %collective-permute-start.2 = (bf16[128,1152]{1,0:T(8,128)(2,1)S(1)}, bf16[128,1152]{1,0:T(8,128)(2,1)S(1)}, u32[]{:S(2)}, u32[]{:S(2)}) collective-permute-start(bf16[128,1152]{1,0:T(8,128)(2,1)S(1)} %get-tuple-element.16), channel_id=1, source_target_pairs={{0,1},{1,0},{2,3},{3,2},{4,5},{5,4},{6,7},{7,6},{8,9},{9,8},{10,11... | collective-permute-start | bytes 884744 | tf_op jit(solution)/shard_map/ppermute | solution.py:174
  51.6 1.2 collective-permute-done.2.recv_ref
  52.8 0.3 scatter.1
  53.0 0.0 copy-start.5
  53.0 2.1 %collective-permute-start.3 = (bf16[32,1152]{1,0:T(8,128)(2,1)S(1)}, bf16[32,1152]{1,0:T(8,128)(2,1)S(1)}, u32[]{:S(2)}, u32[]{:S(2)}) collective-permute-start(bf16[32,1152]{1,0:T(8,128)(2,1)S(1)} %get-tuple-element.18), channel_id=1, source_target_pairs={{0,2},{1,3},{2,0},{3,1},{4,6},{5,7},{6,4},{7,5},{8,10},{9,11},{10,... | collective-permute-start | bytes 221192 | tf_op jit(solution)/shard_map/ppermute | solution.py:174
  55.1 2.8 %collective-permute-start.4 = (bf16[32,1152]{1,0:T(8,128)(2,1)S(1)}, bf16[32,1152]{1,0:T(8,128)(2,1)S(1)}, u32[]{:S(2)}, u32[]{:S(2)}) collective-permute-start(bf16[32,1152]{1,0:T(8,128)(2,1)S(1)} %get-tuple-element.19), channel_id=1, source_target_pairs={{0,4},{1,5},{2,6},{3,7},{4,0},{5,1},{6,2},{7,3},{8,12},{9,13},{10,... | collective-permute-start | bytes 221192 | tf_op jit(solution)/shard_map/ppermute | solution.py:174
  57.9 4.6 %collective-permute-start.5 = (bf16[32,1152]{1,0:T(8,128)(2,1)S(1)}, bf16[32,1152]{1,0:T(8,128)(2,1)S(1)}, u32[]{:S(2)}, u32[]{:S(2)}) collective-permute-start(bf16[32,1152]{1,0:T(8,128)(2,1)S(1)} %get-tuple-element.20), channel_id=1, source_target_pairs={{0,6},{1,7},{2,4},{3,5},{4,2},{5,3},{6,0},{7,1},{8,14},{9,15},{10,... | collective-permute-start | bytes 221192 | tf_op jit(solution)/shard_map/ppermute | solution.py:174
  62.5 0.0 collective-permute-done.3.one_ref
  62.5 0.0 collective-permute-done.4.two_ref
  62.5 3.3 %collective-permute-done.5.three_ref = bf16[32,1152]{1,0:T(8,128)(2,1)S(1)} collective-permute-done((bf16[32,1152]{1,0:T(8,128)(2,1)S(1)}, bf16[32,1152]{1,0:T(8,128)(2,1)S(1)}, u32[]{:S(2)}, u32[]{:S(2)}) %collective-permute-start.5) | collective-permute-done | bytes 73760 | tf_op jit(solution)/shard_map/ppermute | solution.py:174
  65.8 0.0 copy-done.9
  65.8 0.5 step.1
  66.3 2.1 %collective-permute-start.6 = (bf16[32,512]{1,0:T(8,128)(2,1)S(1)}, bf16[32,512]{1,0:T(8,128)(2,1)S(1)}, u32[]{:S(2)}, u32[]{:S(2)}) collective-permute-start(bf16[32,512]{1,0:T(8,128)(2,1)S(1)} %get-tuple-element.22), channel_id=1, source_target_pairs={{0,504},{8,496},{16,488},{24,480},{32,472},{40,464},{48,456},{56,4... | collective-permute-start | bytes 98312 | tf_op jit(solution)/shard_map/ppermute | solution.py:206
  68.4 0.0 copy-start.3
  68.4 11.1 %collective-permute-done.6 = bf16[32,512]{1,0:T(8,128)(2,1)S(1)} collective-permute-done((bf16[32,512]{1,0:T(8,128)(2,1)S(1)}, bf16[32,512]{1,0:T(8,128)(2,1)S(1)}, u32[]{:S(2)}, u32[]{:S(2)}) %collective-permute-start.6) | collective-permute-done | bytes 32800 | tf_op jit(solution)/shard_map/ppermute | solution.py:206
  79.5 3.5 %collective-permute-start.9 = (bf16[32,1408]{1,0:T(8,128)(2,1)S(1)}, bf16[32,1408]{1,0:T(8,128)(2,1)S(1)}, u32[]{:S(2)}, u32[]{:S(2)}) collective-permute-start(bf16[32,1408]{1,0:T(8,128)(2,1)S(1)} %constant_dynamic-update-slice_fusion.own_ref), channel_id=1, source_target_pairs={{0,6},{1,7},{2,4},{3,5},{4,2},{5,3},{6,0},{7,1},{8,14},{9,15},{10,... | collective-permute-start | bytes 270344 | tf_op jit(solution)/shard_map/ppermute | solution.py:174
  83.0 4.0 %collective-permute-start.8 = (bf16[32,1408]{1,0:T(8,128)(2,1)S(1)}, bf16[32,1408]{1,0:T(8,128)(2,1)S(1)}, u32[]{:S(2)}, u32[]{:S(2)}) collective-permute-start(bf16[32,1408]{1,0:T(8,128)(2,1)S(1)} %constant_dynamic-update-slice_fusion.own_ref), channel_id=1, source_target_pairs={{0,4},{1,5},{2,6},{3,7},{4,0},{5,1},{6,2},{7,3},{8,12},{9,13},{10,... | collective-permute-start | bytes 270344 | tf_op jit(solution)/shard_map/ppermute | solution.py:174
  87.0 1.9 %collective-permute-start.7 = (bf16[32,1408]{1,0:T(8,128)(2,1)S(1)}, bf16[32,1408]{1,0:T(8,128)(2,1)S(1)}, u32[]{:S(2)}, u32[]{:S(2)}) collective-permute-start(bf16[32,1408]{1,0:T(8,128)(2,1)S(1)} %constant_dynamic-update-slice_fusion.own_ref), channel_id=1, source_target_pairs={{0,2},{1,3},{2,0},{3,1},{4,6},{5,7},{6,4},{7,5},{8,10},{9,11},{10,... | collective-permute-start | bytes 270344 | tf_op jit(solution)/shard_map/ppermute | solution.py:174
  88.9 0.0 copy-done.10
  88.9 1.9 %collective-permute-start.12 = (bf16[1,224,896]{2,1,0:T(8,128)(2,1)S(1)}, bf16[1,224,896]{2,1,0:T(8,128)(2,1)S(1)}, u32[]{:S(2)}, u32[]{:S(2)}) collective-permute-start(bf16[1,224,896]{2,1,0:T(8,128)(2,1)S(1)} %copy-done.10), channel_id=1, source_target_pairs={{0,496},{8,488},{16,480},{24,472},{32,464},{40,456},{48,448},{56,4... | collective-permute-start | bytes 1204232 | tf_op jit(solution)/shard_map/ppermute | solution.py:179
  90.8 0.0 copy-done.5
  90.9 1.9 %collective-permute-start.11 = (bf16[1,224,896]{2,1,0:T(8,128)(2,1)S(1)}, bf16[1,224,896]{2,1,0:T(8,128)(2,1)S(1)}, u32[]{:S(2)}, u32[]{:S(2)}) collective-permute-start(bf16[1,224,896]{2,1,0:T(8,128)(2,1)S(1)} %copy-done.5), channel_id=1, source_target_pairs={{0,504},{8,496},{16,488},{24,480},{32,472},{40,464},{48,456},{56,4... | collective-permute-start | bytes 1204232 | tf_op jit(solution)/shard_map/ppermute | solution.py:178
  92.8 30.9 %collective-permute-done.9.three_ref = bf16[32,1408]{1,0:T(8,128)(2,1)S(1)} collective-permute-done((bf16[32,1408]{1,0:T(8,128)(2,1)S(1)}, bf16[32,1408]{1,0:T(8,128)(2,1)S(1)}, u32[]{:S(2)}, u32[]{:S(2)}) %collective-permute-start.9) | collective-permute-done | bytes 90144 | tf_op jit(solution)/shard_map/ppermute | solution.py:174
  123.7 4.0 %collective-permute-done.8.two_ref = bf16[32,1408]{1,0:T(8,128)(2,1)S(1)} collective-permute-done((bf16[32,1408]{1,0:T(8,128)(2,1)S(1)}, bf16[32,1408]{1,0:T(8,128)(2,1)S(1)}, u32[]{:S(2)}, u32[]{:S(2)}) %collective-permute-start.8) | collective-permute-done | bytes 90144 | tf_op jit(solution)/shard_map/ppermute | solution.py:174
  127.7 0.0 collective-permute-done.7.one_ref
  127.8 2.4 %collective-permute-start.10 = (bf16[128,1408]{1,0:T(8,128)(2,1)S(1)}, bf16[128,1408]{1,0:T(8,128)(2,1)S(1)}, u32[]{:S(2)}, u32[]{:S(2)}) collective-permute-start(bf16[128,1408]{1,0:T(8,128)(2,1)S(1)} %gather.1.mine_ref), channel_id=1, source_target_pairs={{0,1},{1,0},{2,3},{3,2},{4,5},{5,4},{6,7},{7,6},{8,9},{9,8},{10,11... | collective-permute-start | bytes 1081352 | tf_op jit(solution)/shard_map/ppermute | solution.py:174
  130.2 0.0 collective-permute-done.12.cm_ref
  130.2 9.5 %collective-permute-done.11.xm_ref = bf16[1,224,896]{2,1,0:T(8,128)(2,1)S(1)} collective-permute-done((bf16[1,224,896]{2,1,0:T(8,128)(2,1)S(1)}, bf16[1,224,896]{2,1,0:T(8,128)(2,1)S(1)}, u32[]{:S(2)}, u32[]{:S(2)}) %collective-permute-start.11) | collective-permute-done | bytes 401440 | tf_op jit(solution)/shard_map/ppermute | solution.py:178
  139.7 0.0 collective-permute-done.10.other_ref
  139.7 0.0 copy-done.1
  139.7 0.0 copy-done.3
  139.7 0.0 copy-done.8
  139.7 2.3 %finish.1 = (bf16[1,224,896]{2,1,0:T(8,128)(2,1)}, bf16[1,224,896]{2,1,0:T(8,128)(2,1)}, bf16[1,256,896]{2,1,0:T(8,128)(2,1)}, bf16[1,256,896]{2,1,0:T(8,128)(2,1)}) custom-call(bf16[128,1408]{1,0:T(8,128)(2,1)S(1)} %gather.1.mine_ref, bf16[128,1408]{1,0:T(8,128)(2,1)S(1)} %collective-permute-done.10.other_ref, ...), custom_call_target="tpu_custom_call" | custom-call | flops 616562688 | bytes 4194304 | tf_op jit(solution)/shard_map/finish/pallas_call | solution.py:215
  (8 shorter events, 0.1 us)
Async XLA Ops:
  0.6 29.8 %collective-permute-start = (bf16[1,224,896]{2,1,0:T(8,128)(2,1)}, bf16[1,224,896]{2,1,0:T(8,128)(2,1)S(1)}, u32[]{:S(2)}, u32[]{:S(2)}) collective-permute-start(bf16[1,224,896]{2,1,0:T(8,128)(2,1)} %param.10), channel_id=1, source_target_pairs={{8,0},{16,8},{24,16},{32,24},{40,32},{48,40},{56,48},{64,56},{72,6... | collective-permute-start | bytes 1204232 | tf_op jit(solution)/shard_map/ppermute | solution.py:176
  17.2 28.6 %collective-permute-start.1 = (bf16[1,224,896]{2,1,0:T(8,128)(2,1)}, bf16[1,224,896]{2,1,0:T(8,128)(2,1)S(1)}, u32[]{:S(2)}, u32[]{:S(2)}) collective-permute-start(bf16[1,224,896]{2,1,0:T(8,128)(2,1)} %param.11), channel_id=1, source_target_pairs={{0,8},{8,16},{16,24},{24,32},{32,40},{40,48},{48,56},{56,64},{64,7... | collective-permute-start | bytes 1204232 | tf_op jit(solution)/shard_map/ppermute | solution.py:177
  19.1 1.2 copy-start
  20.3 1.0 copy-start.2
  21.3 1.0 copy-start.4
  22.3 0.7 copy-start.7
  23.0 22.8 %copy-start.6 = (bf16[1,2,256,896]{3,2,1,0:T(8,128)(2,1)S(1)}, bf16[1,2,256,896]{3,2,1,0:T(8,128)(2,1)}, u32[]{:S(2)}) copy-start(bf16[1,2,256,896]{3,2,1,0:T(8,128)(2,1)} %we_ref.1) | copy-start | bytes 2752516
  45.8 43.1 %copy-start.10 = (bf16[1,224,896]{2,1,0:T(8,128)(2,1)S(1)}, bf16[1,224,896]{2,1,0:T(8,128)(2,1)}, u32[]{:S(2)}) copy-start(bf16[1,224,896]{2,1,0:T(8,128)(2,1)} %param.11) | copy-start | bytes 1204228
  46.4 6.4 %collective-permute-start.2 = (bf16[128,1152]{1,0:T(8,128)(2,1)S(1)}, bf16[128,1152]{1,0:T(8,128)(2,1)S(1)}, u32[]{:S(2)}, u32[]{:S(2)}) collective-permute-start(bf16[128,1152]{1,0:T(8,128)(2,1)S(1)} %get-tuple-element.16), channel_id=1, source_target_pairs={{0,1},{1,0},{2,3},{3,2},{4,5},{5,4},{6,7},{7,6},{8,9},{9,8},{10,11... | collective-permute-start | bytes 884744 | tf_op jit(solution)/shard_map/ppermute | solution.py:174
  52.8 13.0 %copy-start.9 = (f32[1,2,256]{2,1,0:T(2,128)S(1)}, f32[1,2,256]{2,1,0:T(2,128)}, u32[]{:S(2)}) copy-start(f32[1,2,256]{2,1,0:T(2,128)} %gain_ref.4) | copy-start | bytes 6148
  52.8 86.9 %copy-start.1 = (bf16[1,2,256,896]{3,2,1,0:T(8,128)(2,1)S(1)}, bf16[1,2,256,896]{3,2,1,0:T(8,128)(2,1)}, u32[]{:S(2)}) copy-start(bf16[1,2,256,896]{3,2,1,0:T(8,128)(2,1)} %wc_ref.3) | copy-start | bytes 2752516
  53.0 37.8 %copy-start.5 = (bf16[1,224,896]{2,1,0:T(8,128)(2,1)S(1)}, bf16[1,224,896]{2,1,0:T(8,128)(2,1)}, u32[]{:S(2)}) copy-start(bf16[1,224,896]{2,1,0:T(8,128)(2,1)} %xb_ref.3) | copy-start | bytes 1204228
  53.0 9.4 %collective-permute-start.3 = (bf16[32,1152]{1,0:T(8,128)(2,1)S(1)}, bf16[32,1152]{1,0:T(8,128)(2,1)S(1)}, u32[]{:S(2)}, u32[]{:S(2)}) collective-permute-start(bf16[32,1152]{1,0:T(8,128)(2,1)S(1)} %get-tuple-element.18), channel_id=1, source_target_pairs={{0,2},{1,3},{2,0},{3,1},{4,6},{5,7},{6,4},{7,5},{8,10},{9,11},{10,... | collective-permute-start | bytes 221192 | tf_op jit(solution)/shard_map/ppermute | solution.py:174
  55.1 7.4 %collective-permute-start.4 = (bf16[32,1152]{1,0:T(8,128)(2,1)S(1)}, bf16[32,1152]{1,0:T(8,128)(2,1)S(1)}, u32[]{:S(2)}, u32[]{:S(2)}) collective-permute-start(bf16[32,1152]{1,0:T(8,128)(2,1)S(1)} %get-tuple-element.19), channel_id=1, source_target_pairs={{0,4},{1,5},{2,6},{3,7},{4,0},{5,1},{6,2},{7,3},{8,12},{9,13},{10,... | collective-permute-start | bytes 221192 | tf_op jit(solution)/shard_map/ppermute | solution.py:174
  57.9 7.9 %collective-permute-start.5 = (bf16[32,1152]{1,0:T(8,128)(2,1)S(1)}, bf16[32,1152]{1,0:T(8,128)(2,1)S(1)}, u32[]{:S(2)}, u32[]{:S(2)}) collective-permute-start(bf16[32,1152]{1,0:T(8,128)(2,1)S(1)} %get-tuple-element.20), channel_id=1, source_target_pairs={{0,6},{1,7},{2,4},{3,5},{4,2},{5,3},{6,0},{7,1},{8,14},{9,15},{10,... | collective-permute-start | bytes 221192 | tf_op jit(solution)/shard_map/ppermute | solution.py:174
  66.3 13.2 %collective-permute-start.6 = (bf16[32,512]{1,0:T(8,128)(2,1)S(1)}, bf16[32,512]{1,0:T(8,128)(2,1)S(1)}, u32[]{:S(2)}, u32[]{:S(2)}) collective-permute-start(bf16[32,512]{1,0:T(8,128)(2,1)S(1)} %get-tuple-element.22), channel_id=1, source_target_pairs={{0,504},{8,496},{16,488},{24,480},{32,472},{40,464},{48,456},{56,4... | collective-permute-start | bytes 98312 | tf_op jit(solution)/shard_map/ppermute | solution.py:206
  68.4 71.3 %copy-start.3 = (bf16[1,224,896]{2,1,0:T(8,128)(2,1)S(1)}, bf16[1,224,896]{2,1,0:T(8,128)(2,1)}, u32[]{:S(2)}) copy-start(bf16[1,224,896]{2,1,0:T(8,128)(2,1)} %xa_ref.3) | copy-start | bytes 1204228
  79.5 60.2 %copy-start.8 = (f32[1,2,896]{2,1,0:T(2,128)S(1)}, f32[1,2,896]{2,1,0:T(2,128)}, u32[]{:S(2)}) copy-start(f32[1,2,896]{2,1,0:T(2,128)} %gain_ref.5) | copy-start | bytes 21508
  79.5 44.2 %collective-permute-start.9 = (bf16[32,1408]{1,0:T(8,128)(2,1)S(1)}, bf16[32,1408]{1,0:T(8,128)(2,1)S(1)}, u32[]{:S(2)}, u32[]{:S(2)}) collective-permute-start(bf16[32,1408]{1,0:T(8,128)(2,1)S(1)} %constant_dynamic-update-slice_fusion.own_ref), channel_id=1, source_target_pairs={{0,6},{1,7},{2,4},{3,5},{4,2},{5,3},{6,0},{7,1},{8,14},{9,15},{10,... | collective-permute-start | bytes 270344 | tf_op jit(solution)/shard_map/ppermute | solution.py:174
  83.0 44.7 %collective-permute-start.8 = (bf16[32,1408]{1,0:T(8,128)(2,1)S(1)}, bf16[32,1408]{1,0:T(8,128)(2,1)S(1)}, u32[]{:S(2)}, u32[]{:S(2)}) collective-permute-start(bf16[32,1408]{1,0:T(8,128)(2,1)S(1)} %constant_dynamic-update-slice_fusion.own_ref), channel_id=1, source_target_pairs={{0,4},{1,5},{2,6},{3,7},{4,0},{5,1},{6,2},{7,3},{8,12},{9,13},{10,... | collective-permute-start | bytes 270344 | tf_op jit(solution)/shard_map/ppermute | solution.py:174
  87.0 40.7 %collective-permute-start.7 = (bf16[32,1408]{1,0:T(8,128)(2,1)S(1)}, bf16[32,1408]{1,0:T(8,128)(2,1)S(1)}, u32[]{:S(2)}, u32[]{:S(2)}) collective-permute-start(bf16[32,1408]{1,0:T(8,128)(2,1)S(1)} %constant_dynamic-update-slice_fusion.own_ref), channel_id=1, source_target_pairs={{0,2},{1,3},{2,0},{3,1},{4,6},{5,7},{6,4},{7,5},{8,10},{9,11},{10,... | collective-permute-start | bytes 270344 | tf_op jit(solution)/shard_map/ppermute | solution.py:174
  88.9 41.3 %collective-permute-start.12 = (bf16[1,224,896]{2,1,0:T(8,128)(2,1)S(1)}, bf16[1,224,896]{2,1,0:T(8,128)(2,1)S(1)}, u32[]{:S(2)}, u32[]{:S(2)}) collective-permute-start(bf16[1,224,896]{2,1,0:T(8,128)(2,1)S(1)} %copy-done.10), channel_id=1, source_target_pairs={{0,496},{8,488},{16,480},{24,472},{32,464},{40,456},{48,448},{56,4... | collective-permute-start | bytes 1204232 | tf_op jit(solution)/shard_map/ppermute | solution.py:179
  90.9 48.8 %collective-permute-start.11 = (bf16[1,224,896]{2,1,0:T(8,128)(2,1)S(1)}, bf16[1,224,896]{2,1,0:T(8,128)(2,1)S(1)}, u32[]{:S(2)}, u32[]{:S(2)}) collective-permute-start(bf16[1,224,896]{2,1,0:T(8,128)(2,1)S(1)} %copy-done.5), channel_id=1, source_target_pairs={{0,504},{8,496},{16,488},{24,480},{32,472},{40,464},{48,456},{56,4... | collective-permute-start | bytes 1204232 | tf_op jit(solution)/shard_map/ppermute | solution.py:178
  127.8 11.9 %collective-permute-start.10 = (bf16[128,1408]{1,0:T(8,128)(2,1)S(1)}, bf16[128,1408]{1,0:T(8,128)(2,1)S(1)}, u32[]{:S(2)}, u32[]{:S(2)}) collective-permute-start(bf16[128,1408]{1,0:T(8,128)(2,1)S(1)} %gather.1.mine_ref), channel_id=1, source_target_pairs={{0,1},{1,0},{2,3},{3,2},{4,5},{5,4},{6,7},{7,6},{8,9},{9,8},{10,11... | collective-permute-start | bytes 1081352 | tf_op jit(solution)/shard_map/ppermute | solution.py:174

commit v2 on v1

--- a/solution.py
+++ b/solution.py
@@ -175,8 +175,11 @@
 
     ca = lax.ppermute(sent_a, "pipe", [((i + 1) % len(pipe), i) for i in pipe])
     cb = lax.ppermute(sent_b, "pipe", [(i, (i + 1) % len(pipe)) for i in pipe])
-    xm = lax.ppermute(xb, "pipe", [(i, last - i) for i in pipe])
-    cm = lax.ppermute(sent_b, "pipe", [(i, (last - 1 - i) % len(pipe)) for i in pipe])
+    half = len(pipe) // 2
+    xm = lax.ppermute(xb, "pipe", [(i, i ^ half) for i in pipe])
+    cm = lax.ppermute(
+        sent_b, "pipe", [(i, i if i % half == half - 1 else i - i % half + half - 2 - i % half) for i in pipe]
+    )
 
     xga, xgb, lat = call(
         latent_kernel,
@@ -203,11 +206,15 @@
         [((PART, OWN_COLS), BF16), ((PART, MIR_COLS), BF16)],
         name="step",
     )(own, *parts, latent_gain)
+    xm, cm, mir = lax.optimization_barrier((xm, cm, mir))
+    xm = lax.ppermute(xm, "pipe", [(i, i ^ (half - 1)) for i in pipe])
+    cm = lax.ppermute(cm, "pipe", [(i, i if i % half == half - 1 else i ^ half) for i in pipe])
     mir = lax.ppermute(mir, "pipe", [(i, last - i) for i in pipe])
     out = jnp.concatenate([out, mir], 1)
     (mine,) = call(gather_kernel, [((HALF, ALL_COLS), BF16)], name="gather")(
         out, *(swap(out, 2 * d) for d in (1, 2, 3))
     )
+    mine, xm, cm = lax.optimization_barrier((mine, xm, cm))
     other = swap(mine, 1)
     big = ((1, TOKENS, WIDTH), BF16)
     grad = ((1, UNITS, WIDTH), BF16)

time: 143 us -> 115 us (0.80)
  waiting for transfers between devices: 81.6 us -> 45.3 us
  starting transfers between devices: 50.8 us -> 59 us
    ppermute x8, waiting for transfers between devices: 39.4 us -> 16.6 us  [swap(): return lax.ppermute(value, 'tensor', [(i, i ^ d) for i in tensor])]
    ppermute x2 -> x4, waiting for transfers between devices: 9.45 us -> 0.01 us  [the longest x1 0.01 us: shards(): lax.ppermute(sent_b, 'pipe', [(i, i if i % half == half - 1 else i - i %...]
    ppermute x2 -> x4, starting transfers between devices: 3.84 us -> 11.1 us  [the longest x1 4.42 us: shards(): xm = lax.ppermute(xb, 'pipe', [(i, i ^ half) for i in pipe])]
    ppermute x1, waiting for transfers between devices: 15.4 us -> 10.7 us  [shards(): cb = lax.ppermute(sent_b, 'pipe', [(i, (i + 1) % len(pipe)) for i in pipe])]
    ppermute x1, waiting for transfers between devices: 6.29 us -> 9.24 us  [shards(): ca = lax.ppermute(sent_a, 'pipe', [((i + 1) % len(pipe), i) for i in pipe])]
    ppermute x1, waiting for transfers between devices: 11.1 us -> 8.68 us  [shards(): mir = lax.ppermute(mir, 'pipe', [(i, last - i) for i in pipe])]
    ppermute x1, starting transfers between devices: 2.08 us -> 4.07 us  [shards(): mir = lax.ppermute(mir, 'pipe', [(i, last - i) for i in pipe])]
    unnamed x23 -> x21, local copies, waits for them, and re-layouts: 3.9 us -> 3.9 us
  transfers between devices with their start and end apart: 13 -> 15, of which waited for: 8 -> 9; matrix products, arithmetic and copies ran while one was open for 0% -> 0% of each run, Pallas kernels for 1% -> 2%
where the time goes in v2:
time: 115 us; the launch traced here: 114 us
  starting transfers between devices  59 us (51%)
  waiting for transfers between devices  45.3 us (39%)
  Pallas kernels  4.75 us (4%)
  local copies, waits for them, and re-layouts  3.9 us (3%)
    ppermute x8, starting transfers between devices, swap(): return lax.ppermute(value, 'tensor', [(i, i ^ d) for i in tensor])  25.3 us
    ppermute x8, waiting for transfers between devices, swap(): return lax.ppermute(value, 'tensor', [(i, i ^ d) for i in tensor])  16.6 us
    ppermute x1, starting transfers between devices, shards(): ca = lax.ppermute(sent_a, 'pipe', [((i + 1) % len(pipe), i) for i in pipe])  16.6 us
    ppermute x1, waiting for transfers between devices, shards(): cb = lax.ppermute(sent_b, 'pipe', [(i, (i + 1) % len(pipe)) for i in pipe])  10.7 us
    ppermute x1, waiting for transfers between devices, shards(): ca = lax.ppermute(sent_a, 'pipe', [((i + 1) % len(pipe), i) for i in pipe])  9.24 us
    ppermute x1, waiting for transfers between devices, shards(): mir = lax.ppermute(mir, 'pipe', [(i, last - i) for i in pipe])  8.68 us
    ppermute x1, starting transfers between devices, shards(): xm = lax.ppermute(xb, 'pipe', [(i, i ^ half) for i in pipe])  4.42 us
    ppermute x1, starting transfers between devices, shards(): mir = lax.ppermute(mir, 'pipe', [(i, last - i) for i in pipe])  4.07 us
  transfers between devices with their start and end apart: 15, of which 9 were waited for; matrix products, arithmetic and copies ran while one was open for 0% of the time, Pallas kernels for 2%

profile of v2, /device:TPU:1, one launch (start us, length us, event | category | flops | bytes accessed | tf_op | source)
XLA Modules:
  0.0 113.8 jit_solution(5704247573849676365)
XLA Ops:
  0.6 16.6 %collective-permute-start = (bf16[1,224,896]{2,1,0:T(8,128)(2,1)}, bf16[1,224,896]{2,1,0:T(8,128)(2,1)S(1)}, u32[]{:S(2)}, u32[]{:S(2)}) collective-permute-start(bf16[1,224,896]{2,1,0:T(8,128)(2,1)} %param.10), channel_id=1, source_target_pairs={{8,0},{16,8},{24,16},{32,24},{40,32},{48,40},{56,48},{64,56},{72,6... | collective-permute-start | bytes 1204232 | tf_op jit(solution)/shard_map/ppermute | solution.py:176
  17.2 1.9 %collective-permute-start.1 = (bf16[1,224,896]{2,1,0:T(8,128)(2,1)}, bf16[1,224,896]{2,1,0:T(8,128)(2,1)S(1)}, u32[]{:S(2)}, u32[]{:S(2)}) collective-permute-start(bf16[1,224,896]{2,1,0:T(8,128)(2,1)} %param.11), channel_id=1, source_target_pairs={{0,8},{8,16},{16,24},{24,32},{32,40},{40,48},{48,56},{56,64},{64,7... | collective-permute-start | bytes 1204232 | tf_op jit(solution)/shard_map/ppermute | solution.py:177
  19.1 1.9 %collective-permute-start.7 = (bf16[1,224,896]{2,1,0:T(8,128)(2,1)}, bf16[1,224,896]{2,1,0:T(8,128)(2,1)S(1)}, u32[]{:S(2)}, u32[]{:S(2)}) collective-permute-start(bf16[1,224,896]{2,1,0:T(8,128)(2,1)} %param.11), channel_id=1, source_target_pairs={{0,240},{8,232},{16,224},{24,216},{32,208},{40,200},{48,192},{56,1... | collective-permute-start | bytes 1204232 | tf_op jit(solution)/shard_map/ppermute | solution.py:180
  21.1 4.4 %collective-permute-start.6 = (bf16[1,224,896]{2,1,0:T(8,128)(2,1)}, bf16[1,224,896]{2,1,0:T(8,128)(2,1)S(1)}, u32[]{:S(2)}, u32[]{:S(2)}) collective-permute-start(bf16[1,224,896]{2,1,0:T(8,128)(2,1)} %xb_ref.3), channel_id=1, source_target_pairs={{0,256},{8,264},{16,272},{24,280},{32,288},{40,296},{48,304},{56,3... | collective-permute-start | bytes 1204232 | tf_op jit(solution)/shard_map/ppermute | solution.py:179
  25.5 0.0 copy-start
  25.5 1.2 %copy-done = bf16[1,2,256,896]{3,2,1,0:T(8,128)(2,1)S(1)} copy-done((bf16[1,2,256,896]{3,2,1,0:T(8,128)(2,1)S(1)}, bf16[1,2,256,896]{3,2,1,0:T(8,128)(2,1)}, u32[]{:S(2)}) %copy-start) | copy-done | bytes 917528
  26.7 1.0 copy-done.2
  27.7 1.0 copy-done.4
  28.7 0.7 copy-done.7
  29.4 1.2 %latent.1 = (bf16[224,896]{1,0:T(8,128)(2,1)S(1)}, bf16[224,896]{1,0:T(8,128)(2,1)}, f32[256,640]{1,0:T(8,128)S(1)}) custom-call(bf16[1,224,896]{2,1,0:T(8,128)(2,1)S(1)} %copy-done.2, bf16[1,224,896]{2,1,0:T(8,128)(2,1)S(1)} %copy-done.4, f32[1,2,896]{2,1,0:T(2,128)S(1)} %copy-done.7, bf16[1,2,256,896]{3,2,1,0:T(8,128)(2,1)S(1)} %copy-done), custom_call_target="tpu_custom_call" | custom-call | flops 205520896 | bytes 4194304 | tf_op jit(solution)/shard_map/latent/pallas_call | solution.py:184
  30.5 9.2 %collective-permute-done.ca_ref = bf16[1,224,896]{2,1,0:T(8,128)(2,1)S(1)} collective-permute-done((bf16[1,224,896]{2,1,0:T(8,128)(2,1)}, bf16[1,224,896]{2,1,0:T(8,128)(2,1)S(1)}, u32[]{:S(2)}, u32[]{:S(2)}) %collective-permute-start) | collective-permute-done | bytes 401440 | tf_op jit(solution)/shard_map/ppermute | solution.py:176
  39.8 10.7 %collective-permute-done.1.cb_ref = bf16[1,224,896]{2,1,0:T(8,128)(2,1)S(1)} collective-permute-done((bf16[1,224,896]{2,1,0:T(8,128)(2,1)}, bf16[1,224,896]{2,1,0:T(8,128)(2,1)S(1)}, u32[]{:S(2)}, u32[]{:S(2)}) %collective-permute-start.1) | collective-permute-done | bytes 401440 | tf_op jit(solution)/shard_map/ppermute | solution.py:177
  50.5 0.0 copy-done.6
  50.5 0.5 code.1
  51.0 3.9 %collective-permute-start.2 = (bf16[128,1152]{1,0:T(8,128)(2,1)S(1)}, bf16[128,1152]{1,0:T(8,128)(2,1)S(1)}, u32[]{:S(2)}, u32[]{:S(2)}) collective-permute-start(bf16[128,1152]{1,0:T(8,128)(2,1)S(1)} %get-tuple-element.22), channel_id=1, source_target_pairs={{0,1},{1,0},{2,3},{3,2},{4,5},{5,4},{6,7},{7,6},{8,9},{9,8},{10,11... | collective-permute-start | bytes 884744 | tf_op jit(solution)/shard_map/ppermute | solution.py:174
  55.0 1.2 %collective-permute-done.2.recv_ref = bf16[128,1152]{1,0:T(8,128)(2,1)S(1)} collective-permute-done((bf16[128,1152]{1,0:T(8,128)(2,1)S(1)}, bf16[128,1152]{1,0:T(8,128)(2,1)S(1)}, u32[]{:S(2)}, u32[]{:S(2)}) %collective-permute-start.2) | collective-permute-done | bytes 294944 | tf_op jit(solution)/shard_map/ppermute | solution.py:174
  56.2 0.3 scatter.1
  56.4 3.2 %collective-permute-start.3 = (bf16[32,1152]{1,0:T(8,128)(2,1)S(1)}, bf16[32,1152]{1,0:T(8,128)(2,1)S(1)}, u32[]{:S(2)}, u32[]{:S(2)}) collective-permute-start(bf16[32,1152]{1,0:T(8,128)(2,1)S(1)} %get-tuple-element.24), channel_id=1, source_target_pairs={{0,2},{1,3},{2,0},{3,1},{4,6},{5,7},{6,4},{7,5},{8,10},{9,11},{10,... | collective-permute-start | bytes 221192 | tf_op jit(solution)/shard_map/ppermute | solution.py:174
  59.7 4.4 %collective-permute-start.4 = (bf16[32,1152]{1,0:T(8,128)(2,1)S(1)}, bf16[32,1152]{1,0:T(8,128)(2,1)S(1)}, u32[]{:S(2)}, u32[]{:S(2)}) collective-permute-start(bf16[32,1152]{1,0:T(8,128)(2,1)S(1)} %get-tuple-element.25), channel_id=1, source_target_pairs={{0,4},{1,5},{2,6},{3,7},{4,0},{5,1},{6,2},{7,3},{8,12},{9,13},{10,... | collective-permute-start | bytes 221192 | tf_op jit(solution)/shard_map/ppermute | solution.py:174
  64.1 1.9 %collective-permute-start.5 = (bf16[32,1152]{1,0:T(8,128)(2,1)S(1)}, bf16[32,1152]{1,0:T(8,128)(2,1)S(1)}, u32[]{:S(2)}, u32[]{:S(2)}) collective-permute-start(bf16[32,1152]{1,0:T(8,128)(2,1)S(1)} %get-tuple-element.26), channel_id=1, source_target_pairs={{0,6},{1,7},{2,4},{3,5},{4,2},{5,3},{6,0},{7,1},{8,14},{9,15},{10,... | collective-permute-start | bytes 221192 | tf_op jit(solution)/shard_map/ppermute | solution.py:174
  66.0 0.0 collective-permute-done.3.one_ref
  66.1 2.0 %collective-permute-done.4.two_ref = bf16[32,1152]{1,0:T(8,128)(2,1)S(1)} collective-permute-done((bf16[32,1152]{1,0:T(8,128)(2,1)S(1)}, bf16[32,1152]{1,0:T(8,128)(2,1)S(1)}, u32[]{:S(2)}, u32[]{:S(2)}) %collective-permute-start.4) | collective-permute-done | bytes 73760 | tf_op jit(solution)/shard_map/ppermute | solution.py:174
  68.0 3.0 %collective-permute-done.5.three_ref = bf16[32,1152]{1,0:T(8,128)(2,1)S(1)} collective-permute-done((bf16[32,1152]{1,0:T(8,128)(2,1)S(1)}, bf16[32,1152]{1,0:T(8,128)(2,1)S(1)}, u32[]{:S(2)}, u32[]{:S(2)}) %collective-permute-start.5) | collective-permute-done | bytes 73760 | tf_op jit(solution)/shard_map/ppermute | solution.py:174
  71.0 0.0 copy-done.9
  71.0 0.5 step.1
  71.5 0.0 collective-permute-done.7
  71.5 0.0 collective-permute-done.6
  71.5 1.9 %collective-permute-start.12 = (bf16[1,224,896]{2,1,0:T(8,128)(2,1)S(1)}, bf16[1,224,896]{2,1,0:T(8,128)(2,1)S(1)}, u32[]{:S(2)}, u32[]{:S(2)}) collective-permute-start(bf16[1,224,896]{2,1,0:T(8,128)(2,1)S(1)} %collective-permute-done.6), channel_id=1, source_target_pairs={{0,248},{8,240},{16,232},{24,224},{32,216},{40,208},{48,200},{56,1... | collective-permute-start | bytes 1204232 | tf_op jit(solution)/shard_map/ppermute | solution.py:210
  73.5 2.9 %collective-permute-start.13 = (bf16[1,224,896]{2,1,0:T(8,128)(2,1)S(1)}, bf16[1,224,896]{2,1,0:T(8,128)(2,1)S(1)}, u32[]{:S(2)}, u32[]{:S(2)}) collective-permute-start(bf16[1,224,896]{2,1,0:T(8,128)(2,1)S(1)} %collective-permute-done.7), channel_id=1, source_target_pairs={{0,256},{8,264},{16,272},{24,280},{32,288},{40,296},{48,304},{56,3... | collective-permute-start | bytes 1204232 | tf_op jit(solution)/shard_map/ppermute | solution.py:211
  76.4 4.1 %collective-permute-start.8 = (bf16[32,512]{1,0:T(8,128)(2,1)S(1)}, bf16[32,512]{1,0:T(8,128)(2,1)S(1)}, u32[]{:S(2)}, u32[]{:S(2)}) collective-permute-start(bf16[32,512]{1,0:T(8,128)(2,1)S(1)} %get-tuple-element.29), channel_id=1, source_target_pairs={{0,504},{8,496},{16,488},{24,480},{32,472},{40,464},{48,456},{56,4... | collective-permute-start | bytes 98312 | tf_op jit(solution)/shard_map/ppermute | solution.py:212
  80.4 0.0 copy-start.5
  80.5 0.0 copy-start.3
  80.5 8.7 %collective-permute-done.8 = bf16[32,512]{1,0:T(8,128)(2,1)S(1)} collective-permute-done((bf16[32,512]{1,0:T(8,128)(2,1)S(1)}, bf16[32,512]{1,0:T(8,128)(2,1)S(1)}, u32[]{:S(2)}, u32[]{:S(2)}) %collective-permute-start.8) | collective-permute-done | bytes 32800 | tf_op jit(solution)/shard_map/ppermute | solution.py:212
  89.2 2.8 %collective-permute-start.11 = (bf16[32,1408]{1,0:T(8,128)(2,1)S(1)}, bf16[32,1408]{1,0:T(8,128)(2,1)S(1)}, u32[]{:S(2)}, u32[]{:S(2)}) collective-permute-start(bf16[32,1408]{1,0:T(8,128)(2,1)S(1)} %constant_dynamic-update-slice_fusion.own_ref), channel_id=1, source_target_pairs={{0,6},{1,7},{2,4},{3,5},{4,2},{5,3},{6,0},{7,1},{8,14},{9,15},{10,... | collective-permute-start | bytes 270344 | tf_op jit(solution)/shard_map/ppermute | solution.py:174
  92.0 3.1 %collective-permute-start.10 = (bf16[32,1408]{1,0:T(8,128)(2,1)S(1)}, bf16[32,1408]{1,0:T(8,128)(2,1)S(1)}, u32[]{:S(2)}, u32[]{:S(2)}) collective-permute-start(bf16[32,1408]{1,0:T(8,128)(2,1)S(1)} %constant_dynamic-update-slice_fusion.own_ref), channel_id=1, source_target_pairs={{0,4},{1,5},{2,6},{3,7},{4,0},{5,1},{6,2},{7,3},{8,12},{9,13},{10,... | collective-permute-start | bytes 270344 | tf_op jit(solution)/shard_map/ppermute | solution.py:174
  95.1 3.5 %collective-permute-start.9 = (bf16[32,1408]{1,0:T(8,128)(2,1)S(1)}, bf16[32,1408]{1,0:T(8,128)(2,1)S(1)}, u32[]{:S(2)}, u32[]{:S(2)}) collective-permute-start(bf16[32,1408]{1,0:T(8,128)(2,1)S(1)} %constant_dynamic-update-slice_fusion.own_ref), channel_id=1, source_target_pairs={{0,2},{1,3},{2,0},{3,1},{4,6},{5,7},{6,4},{7,5},{8,10},{9,11},{10,... | collective-permute-start | bytes 270344 | tf_op jit(solution)/shard_map/ppermute | solution.py:174
  98.6 3.3 %collective-permute-done.11.three_ref = bf16[32,1408]{1,0:T(8,128)(2,1)S(1)} collective-permute-done((bf16[32,1408]{1,0:T(8,128)(2,1)S(1)}, bf16[32,1408]{1,0:T(8,128)(2,1)S(1)}, u32[]{:S(2)}, u32[]{:S(2)}) %collective-permute-start.11) | collective-permute-done | bytes 90144 | tf_op jit(solution)/shard_map/ppermute | solution.py:174
  101.9 5.9 %collective-permute-done.10.two_ref = bf16[32,1408]{1,0:T(8,128)(2,1)S(1)} collective-permute-done((bf16[32,1408]{1,0:T(8,128)(2,1)S(1)}, bf16[32,1408]{1,0:T(8,128)(2,1)S(1)}, u32[]{:S(2)}, u32[]{:S(2)}) %collective-permute-start.10) | collective-permute-done | bytes 90144 | tf_op jit(solution)/shard_map/ppermute | solution.py:174
  107.7 0.0 collective-permute-done.9.one_ref
  107.8 0.0 collective-permute-done.12.xm_ref
  107.8 0.0 collective-permute-done.13.cm_ref
  107.8 2.4 %collective-permute-start.14 = (bf16[128,1408]{1,0:T(8,128)(2,1)S(1)}, bf16[128,1408]{1,0:T(8,128)(2,1)S(1)}, u32[]{:S(2)}, u32[]{:S(2)}) collective-permute-start(bf16[128,1408]{1,0:T(8,128)(2,1)S(1)} %gather.1.mine_ref), channel_id=1, source_target_pairs={{0,1},{1,0},{2,3},{3,2},{4,5},{5,4},{6,7},{7,6},{8,9},{9,8},{10,11... | collective-permute-start | bytes 1081352 | tf_op jit(solution)/shard_map/ppermute | solution.py:174
  110.2 1.3 %collective-permute-done.14.other_ref = bf16[128,1408]{1,0:T(8,128)(2,1)S(1)} collective-permute-done((bf16[128,1408]{1,0:T(8,128)(2,1)S(1)}, bf16[128,1408]{1,0:T(8,128)(2,1)S(1)}, u32[]{:S(2)}, u32[]{:S(2)}) %collective-permute-start.14) | collective-permute-done | bytes 360480 | tf_op jit(solution)/shard_map/ppermute | solution.py:174
  111.5 0.0 copy-done.1
  111.5 0.0 copy-done.5
  111.5 0.0 copy-done.3
  111.5 0.0 copy-done.8
  111.5 2.3 %finish.1 = (bf16[1,224,896]{2,1,0:T(8,128)(2,1)}, bf16[1,224,896]{2,1,0:T(8,128)(2,1)}, bf16[1,256,896]{2,1,0:T(8,128)(2,1)}, bf16[1,256,896]{2,1,0:T(8,128)(2,1)}) custom-call(bf16[128,1408]{1,0:T(8,128)(2,1)S(1)} %gather.1.mine_ref, bf16[128,1408]{1,0:T(8,128)(2,1)S(1)} %collective-permute-done.14.other_ref, ...), custom_call_target="tpu_custom_call" | custom-call | flops 616562688 | bytes 4194304 | tf_op jit(solution)/shard_map/finish/pallas_call | solution.py:222
  (10 shorter events, 0.1 us)
Async XLA Ops:
  0.6 39.1 %collective-permute-start = (bf16[1,224,896]{2,1,0:T(8,128)(2,1)}, bf16[1,224,896]{2,1,0:T(8,128)(2,1)S(1)}, u32[]{:S(2)}, u32[]{:S(2)}) collective-permute-start(bf16[1,224,896]{2,1,0:T(8,128)(2,1)} %param.10), channel_id=1, source_target_pairs={{8,0},{16,8},{24,16},{32,24},{40,32},{48,40},{56,48},{64,56},{72,6... | collective-permute-start | bytes 1204232 | tf_op jit(solution)/shard_map/ppermute | solution.py:176
  17.2 33.3 %collective-permute-start.1 = (bf16[1,224,896]{2,1,0:T(8,128)(2,1)}, bf16[1,224,896]{2,1,0:T(8,128)(2,1)S(1)}, u32[]{:S(2)}, u32[]{:S(2)}) collective-permute-start(bf16[1,224,896]{2,1,0:T(8,128)(2,1)} %param.11), channel_id=1, source_target_pairs={{0,8},{8,16},{16,24},{24,32},{32,40},{40,48},{48,56},{56,64},{64,7... | collective-permute-start | bytes 1204232 | tf_op jit(solution)/shard_map/ppermute | solution.py:177
  19.1 52.4 %collective-permute-start.7 = (bf16[1,224,896]{2,1,0:T(8,128)(2,1)}, bf16[1,224,896]{2,1,0:T(8,128)(2,1)S(1)}, u32[]{:S(2)}, u32[]{:S(2)}) collective-permute-start(bf16[1,224,896]{2,1,0:T(8,128)(2,1)} %param.11), channel_id=1, source_target_pairs={{0,240},{8,232},{16,224},{24,216},{32,208},{40,200},{48,192},{56,1... | collective-permute-start | bytes 1204232 | tf_op jit(solution)/shard_map/ppermute | solution.py:180
  21.1 50.5 %collective-permute-start.6 = (bf16[1,224,896]{2,1,0:T(8,128)(2,1)}, bf16[1,224,896]{2,1,0:T(8,128)(2,1)S(1)}, u32[]{:S(2)}, u32[]{:S(2)}) collective-permute-start(bf16[1,224,896]{2,1,0:T(8,128)(2,1)} %xb_ref.3), channel_id=1, source_target_pairs={{0,256},{8,264},{16,272},{24,280},{32,288},{40,296},{48,304},{56,3... | collective-permute-start | bytes 1204232 | tf_op jit(solution)/shard_map/ppermute | solution.py:179
  25.5 1.2 %copy-start = (bf16[1,2,256,896]{3,2,1,0:T(8,128)(2,1)S(1)}, bf16[1,2,256,896]{3,2,1,0:T(8,128)(2,1)}, u32[]{:S(2)}) copy-start(bf16[1,2,256,896]{3,2,1,0:T(8,128)(2,1)} %wc_ref.3) | copy-start | bytes 2752516
  26.7 1.0 copy-start.2
  27.7 1.0 copy-start.4
  28.7 0.7 copy-start.7
  29.4 21.1 %copy-start.6 = (bf16[1,2,256,896]{3,2,1,0:T(8,128)(2,1)S(1)}, bf16[1,2,256,896]{3,2,1,0:T(8,128)(2,1)}, u32[]{:S(2)}) copy-start(bf16[1,2,256,896]{3,2,1,0:T(8,128)(2,1)} %we_ref.1) | copy-start | bytes 2752516
  51.0 5.1 %collective-permute-start.2 = (bf16[128,1152]{1,0:T(8,128)(2,1)S(1)}, bf16[128,1152]{1,0:T(8,128)(2,1)S(1)}, u32[]{:S(2)}, u32[]{:S(2)}) collective-permute-start(bf16[128,1152]{1,0:T(8,128)(2,1)S(1)} %get-tuple-element.22), channel_id=1, source_target_pairs={{0,1},{1,0},{2,3},{3,2},{4,5},{5,4},{6,7},{7,6},{8,9},{9,8},{10,11... | collective-permute-start | bytes 884744 | tf_op jit(solution)/shard_map/ppermute | solution.py:174
  56.2 14.8 %copy-start.9 = (f32[1,2,256]{2,1,0:T(2,128)S(1)}, f32[1,2,256]{2,1,0:T(2,128)}, u32[]{:S(2)}) copy-start(f32[1,2,256]{2,1,0:T(2,128)} %gain_ref.4) | copy-start | bytes 6148
  56.2 55.3 %copy-start.1 = (bf16[1,2,256,896]{3,2,1,0:T(8,128)(2,1)S(1)}, bf16[1,2,256,896]{3,2,1,0:T(8,128)(2,1)}, u32[]{:S(2)}) copy-start(bf16[1,2,256,896]{3,2,1,0:T(8,128)(2,1)} %wc_ref.3) | copy-start | bytes 2752516
  56.4 9.6 %collective-permute-start.3 = (bf16[32,1152]{1,0:T(8,128)(2,1)S(1)}, bf16[32,1152]{1,0:T(8,128)(2,1)S(1)}, u32[]{:S(2)}, u32[]{:S(2)}) collective-permute-start(bf16[32,1152]{1,0:T(8,128)(2,1)S(1)} %get-tuple-element.24), channel_id=1, source_target_pairs={{0,2},{1,3},{2,0},{3,1},{4,6},{5,7},{6,4},{7,5},{8,10},{9,11},{10,... | collective-permute-start | bytes 221192 | tf_op jit(solution)/shard_map/ppermute | solution.py:174
  59.7 8.3 %collective-permute-start.4 = (bf16[32,1152]{1,0:T(8,128)(2,1)S(1)}, bf16[32,1152]{1,0:T(8,128)(2,1)S(1)}, u32[]{:S(2)}, u32[]{:S(2)}) collective-permute-start(bf16[32,1152]{1,0:T(8,128)(2,1)S(1)} %get-tuple-element.25), channel_id=1, source_target_pairs={{0,4},{1,5},{2,6},{3,7},{4,0},{5,1},{6,2},{7,3},{8,12},{9,13},{10,... | collective-permute-start | bytes 221192 | tf_op jit(solution)/shard_map/ppermute | solution.py:174
  64.1 6.9 %collective-permute-start.5 = (bf16[32,1152]{1,0:T(8,128)(2,1)S(1)}, bf16[32,1152]{1,0:T(8,128)(2,1)S(1)}, u32[]{:S(2)}, u32[]{:S(2)}) collective-permute-start(bf16[32,1152]{1,0:T(8,128)(2,1)S(1)} %get-tuple-element.26), channel_id=1, source_target_pairs={{0,6},{1,7},{2,4},{3,5},{4,2},{5,3},{6,0},{7,1},{8,14},{9,15},{10,... | collective-permute-start | bytes 221192 | tf_op jit(solution)/shard_map/ppermute | solution.py:174
  71.5 36.2 %collective-permute-start.12 = (bf16[1,224,896]{2,1,0:T(8,128)(2,1)S(1)}, bf16[1,224,896]{2,1,0:T(8,128)(2,1)S(1)}, u32[]{:S(2)}, u32[]{:S(2)}) collective-permute-start(bf16[1,224,896]{2,1,0:T(8,128)(2,1)S(1)} %collective-permute-done.6), channel_id=1, source_target_pairs={{0,248},{8,240},{16,232},{24,224},{32,216},{40,208},{48,200},{56,1... | collective-permute-start | bytes 1204232 | tf_op jit(solution)/shard_map/ppermute | solution.py:210
  73.5 34.3 %collective-permute-start.13 = (bf16[1,224,896]{2,1,0:T(8,128)(2,1)S(1)}, bf16[1,224,896]{2,1,0:T(8,128)(2,1)S(1)}, u32[]{:S(2)}, u32[]{:S(2)}) collective-permute-start(bf16[1,224,896]{2,1,0:T(8,128)(2,1)S(1)} %collective-permute-done.7), channel_id=1, source_target_pairs={{0,256},{8,264},{16,272},{24,280},{32,288},{40,296},{48,304},{56,3... | collective-permute-start | bytes 1204232 | tf_op jit(solution)/shard_map/ppermute | solution.py:211
  76.4 12.8 %collective-permute-start.8 = (bf16[32,512]{1,0:T(8,128)(2,1)S(1)}, bf16[32,512]{1,0:T(8,128)(2,1)S(1)}, u32[]{:S(2)}, u32[]{:S(2)}) collective-permute-start(bf16[32,512]{1,0:T(8,128)(2,1)S(1)} %get-tuple-element.29), channel_id=1, source_target_pairs={{0,504},{8,496},{16,488},{24,480},{32,472},{40,464},{48,456},{56,4... | collective-permute-start | bytes 98312 | tf_op jit(solution)/shard_map/ppermute | solution.py:212
  80.4 31.1 %copy-start.5 = (bf16[1,224,896]{2,1,0:T(8,128)(2,1)S(1)}, bf16[1,224,896]{2,1,0:T(8,128)(2,1)}, u32[]{:S(2)}) copy-start(bf16[1,224,896]{2,1,0:T(8,128)(2,1)} %xb_ref.3) | copy-start | bytes 1204228
  80.5 31.0 %copy-start.3 = (bf16[1,224,896]{2,1,0:T(8,128)(2,1)S(1)}, bf16[1,224,896]{2,1,0:T(8,128)(2,1)}, u32[]{:S(2)}) copy-start(bf16[1,224,896]{2,1,0:T(8,128)(2,1)} %xa_ref.3) | copy-start | bytes 1204228
  89.1 22.4 %copy-start.8 = (f32[1,2,896]{2,1,0:T(2,128)S(1)}, f32[1,2,896]{2,1,0:T(2,128)}, u32[]{:S(2)}) copy-start(f32[1,2,896]{2,1,0:T(2,128)} %gain_ref.5) | copy-start | bytes 21508
  89.2 12.7 %collective-permute-start.11 = (bf16[32,1408]{1,0:T(8,128)(2,1)S(1)}, bf16[32,1408]{1,0:T(8,128)(2,1)S(1)}, u32[]{:S(2)}, u32[]{:S(2)}) collective-permute-start(bf16[32,1408]{1,0:T(8,128)(2,1)S(1)} %constant_dynamic-update-slice_fusion.own_ref), channel_id=1, source_target_pairs={{0,6},{1,7},{2,4},{3,5},{4,2},{5,3},{6,0},{7,1},{8,14},{9,15},{10,... | collective-permute-start | bytes 270344 | tf_op jit(solution)/shard_map/ppermute | solution.py:174
  92.0 15.8 %collective-permute-start.10 = (bf16[32,1408]{1,0:T(8,128)(2,1)S(1)}, bf16[32,1408]{1,0:T(8,128)(2,1)S(1)}, u32[]{:S(2)}, u32[]{:S(2)}) collective-permute-start(bf16[32,1408]{1,0:T(8,128)(2,1)S(1)} %constant_dynamic-update-slice_fusion.own_ref), channel_id=1, source_target_pairs={{0,4},{1,5},{2,6},{3,7},{4,0},{5,1},{6,2},{7,3},{8,12},{9,13},{10,... | collective-permute-start | bytes 270344 | tf_op jit(solution)/shard_map/ppermute | solution.py:174
  95.1 12.7 %collective-permute-start.9 = (bf16[32,1408]{1,0:T(8,128)(2,1)S(1)}, bf16[32,1408]{1,0:T(8,128)(2,1)S(1)}, u32[]{:S(2)}, u32[]{:S(2)}) collective-permute-start(bf16[32,1408]{1,0:T(8,128)(2,1)S(1)} %constant_dynamic-update-slice_fusion.own_ref), channel_id=1, source_target_pairs={{0,2},{1,3},{2,0},{3,1},{4,6},{5,7},{6,4},{7,5},{8,10},{9,11},{10,... | collective-permute-start | bytes 270344 | tf_op jit(solution)/shard_map/ppermute | solution.py:174
  107.8 3.7 %collective-permute-start.14 = (bf16[128,1408]{1,0:T(8,128)(2,1)S(1)}, bf16[128,1408]{1,0:T(8,128)(2,1)S(1)}, u32[]{:S(2)}, u32[]{:S(2)}) collective-permute-start(bf16[128,1408]{1,0:T(8,128)(2,1)S(1)} %gather.1.mine_ref), channel_id=1, source_target_pairs={{0,1},{1,0},{2,3},{3,2},{4,5},{5,4},{6,7},{7,6},{8,9},{9,8},{10,11... | collective-permute-start | bytes 1081352 | tf_op jit(solution)/shard_map/ppermute | solution.py:174

commit v3 on v1

--- a/solution.py
+++ b/solution.py
@@ -46,12 +46,13 @@
     return block[:, 0:1] + block[:, 2:3], block[:, 1:2] + block[:, 3:4]
 
 
-def latent_kernel(xa_ref, xb_ref, gain_ref, wc_ref, xga_ref, xgb_ref, lat_ref):
+def latent_kernel(xa_ref, xb_ref, gain_ref, wc_ref, xga_ref, lat_ref):
     squares = []
-    for s, (x_ref, xg_ref) in enumerate(((xa_ref, xga_ref), (xb_ref, xgb_ref))):
+    for s, x_ref in enumerate((xa_ref, xb_ref)):
         x = x_ref[0].astype(F32)
         xg = (x * gain_ref[0, s : s + 1, :]).astype(BF16)
-        xg_ref[...] = xg
+        if s == 0:
+            xga_ref[...] = xg
         lat_ref[0:TOKENS, s * UNITS : (s + 1) * UNITS] = contract_last(xg, wc_ref[0, s])
         squares.append(jnp.sum(x * x, -1, keepdims=True))
     lane = lanes(TOKENS)
@@ -60,9 +61,19 @@
     lat_ref[TOKENS:, :] = jnp.zeros((PADDED - TOKENS, 2 * UNITS + 128), F32)
 
 
-def code_kernel(ca_ref, cb_ref, we_ref, lat_ref, keep_ref, send_ref, full):
-    for s, c_ref in enumerate((ca_ref, cb_ref)):
-        full[0:TOKENS, s * UNITS : (s + 1) * UNITS] = contract_last(c_ref[0], we_ref[0, s])
+def place_and_end():
+    half = lax.axis_size("pipe") // 2
+    return lax.rem(lax.axis_index("pipe"), half), half - 1
+
+
+def code_kernel(ca_ref, cb_ref, sa_ref, sb_ref, we_ref, lat_ref, keep_ref, send_ref, full):
+    place, end = place_and_end()
+    full[0:TOKENS, 0:UNITS] = contract_last(
+        jnp.where(place == end, sb_ref[0], ca_ref[0]), we_ref[0, 0]
+    )
+    full[0:TOKENS, UNITS:] = contract_last(
+        jnp.where(place == 0, sa_ref[0], cb_ref[0]), we_ref[0, 1]
+    )
     full[TOKENS:, :] = jnp.zeros((PADDED - TOKENS, 2 * UNITS), F32)
     core = lax.rem(lax.axis_index("tensor"), 2)
     mine = pl.ds(pl.multiple_of(core * HALF, HALF), HALF)
@@ -103,23 +114,41 @@
     return ratio, code, centre
 
 
-def latent_step_kernel(own_ref, one_ref, two_ref, three_ref, gain_ref, out_ref, mir_ref):
+def sum_kernel(own_ref, one_ref, two_ref, three_ref, total_ref, swap_ref):
     total = own_ref[...]
     for ref in (one_ref, two_ref, three_ref):
         total = total + ref[...].astype(F32)
-    square_a, square_b = joined(total[:, 4 * UNITS :])
+    total_ref[...] = total
+    swap_ref[:, 0:UNITS] = total[:, UNITS : 2 * UNITS].astype(BF16)
+    swap_ref[:, UNITS : 2 * UNITS] = total[:, 3 * UNITS : 4 * UNITS].astype(BF16)
+    swap_ref[:, 2 * UNITS : 3 * UNITS] = total[:, 2 * UNITS : 3 * UNITS].astype(BF16)
+    swap_ref[:, 3 * UNITS :] = split_pair(*joined(total[:, 4 * UNITS :]))
+
+
+def latent_step_kernel(total_ref, far_ref, gain_ref, out_ref):
+    place, end = place_and_end()
+    square_a, square_b = joined(total_ref[:, 4 * UNITS :])
+    _, square_m = joined(far_ref[:, 3 * UNITS :])
+    own_a = total_ref[:, 2 * UNITS : 3 * UNITS]
+    own_b = total_ref[:, 3 * UNITS : 4 * UNITS]
+    far_b = far_ref[:, UNITS : 2 * UNITS].astype(F32)
+    far_a = far_ref[:, 2 * UNITS : 3 * UNITS].astype(F32)
+    gain_a, gain_b = gain_ref[0, 0:1, :], gain_ref[0, 1:2, :]
     ratio_a, code_a, centre_a = latent_backward(
-        total[:, 0:UNITS], total[:, 2 * UNITS : 3 * UNITS], square_a, gain_ref[0, 0:1, :]
-    )
-    ratio_b, code_b, centre_b = latent_backward(
-        total[:, UNITS : 2 * UNITS], total[:, 3 * UNITS : 4 * UNITS], square_b, gain_ref[0, 1:2, :]
+        total_ref[:, 0:UNITS], jnp.where(place == end, far_b, own_a), square_a, gain_a
+    )
+    ratio_b, _, centre_b = latent_backward(
+        total_ref[:, UNITS : 2 * UNITS], jnp.where(place == 0, far_a, own_b), square_b, gain_b
+    )
+    ratio_m, code_m, _ = latent_backward(
+        far_ref[:, 0:UNITS].astype(F32), jnp.where(place == end, own_a, far_b), square_m, gain_a
     )
     out_ref[:, 0:UNITS] = ratio_a
     out_ref[:, UNITS : 2 * UNITS] = code_a
     out_ref[:, 2 * UNITS : 3 * UNITS] = ratio_b
-    out_ref[:, 3 * UNITS :] = split_pair(centre_a, centre_b)
-    mir_ref[:, 0:UNITS] = ratio_b
-    mir_ref[:, UNITS:] = code_b
+    out_ref[:, 3 * UNITS : OWN_COLS] = split_pair(centre_a, centre_b)
+    out_ref[:, OWN_COLS : OWN_COLS + UNITS] = ratio_m
+    out_ref[:, OWN_COLS + UNITS :] = code_m
 
 
 def gather_kernel(own_ref, one_ref, two_ref, three_ref, out_ref):
@@ -129,7 +158,8 @@
 
 
 def finish_kernel(
-    mine_ref, other_ref, ca_ref, cb_ref, xa_ref, xb_ref, xga_ref, xm_ref, cm_ref, gain_ref, wc_ref,
+    mine_ref, other_ref, ca_ref, cb_ref, far_a_ref, far_b_ref, xa_ref, xb_ref, xga_ref, xm_ref,
+    cm_ref, gain_ref, wc_ref,
     ia_ref, ib_ref, gc_ref, ge_ref, full,
 ):
     core = lax.rem(lax.axis_index("tensor"), 2)
@@ -141,17 +171,20 @@
     centres = joined(full[0:TOKENS, 3 * UNITS : OWN_COLS])
     ratio_m = full[0:TOKENS, OWN_COLS : OWN_COLS + UNITS]
     code_m = full[0:TOKENS, OWN_COLS + UNITS :]
-    streams = ((ratio_a, ca_ref, xa_ref, ia_ref), (ratio_b, cb_ref, xb_ref, ib_ref))
-    for s, (ratio, c_ref, x_ref, i_ref) in enumerate(streams):
+    place, end = place_and_end()
+    cot_a = jnp.where(place == end, far_a_ref[0], ca_ref[0])
+    cot_b = jnp.where(place == 0, far_b_ref[0], cb_ref[0])
+    streams = ((ratio_a, cot_a, xa_ref, ia_ref), (ratio_b, cot_b, xb_ref, ib_ref))
+    for s, (ratio, cot, x_ref, i_ref) in enumerate(streams):
         grad = jnp.dot(ratio, wc_ref[0, s], preferred_element_type=F32) * gain_ref[0, s : s + 1, :]
         i_ref[0] = (
-            c_ref[0].astype(F32) + (grad - x_ref[0].astype(F32) * centres[s])
+            cot.astype(F32) + (grad - x_ref[0].astype(F32) * centres[s])
         ).astype(BF16)
     xg_m = (xm_ref[0].astype(F32) * gain_ref[0, 0:1, :]).astype(BF16)
     mirror = contract_first(ratio_m, xg_m).astype(BF16).astype(F32)
     gc_ref[0] = (contract_first(ratio_a, xga_ref[...]) + mirror).astype(BF16)
     mirror = contract_first(code_m, cm_ref[0]).astype(BF16).astype(F32)
-    ge_ref[0] = (contract_first(code_a, ca_ref[0]) + mirror).astype(BF16)
+    ge_ref[0] = (contract_first(code_a, cot_a) + mirror).astype(BF16)
 
 
 def call(kernel, outs, scratch=(), flops=0, name=None):
@@ -173,38 +206,69 @@
     def swap(value, d):
         return lax.ppermute(value, "tensor", [(i, i ^ d) for i in tensor])
 
-    ca = lax.ppermute(sent_a, "pipe", [((i + 1) % len(pipe), i) for i in pipe])
-    cb = lax.ppermute(sent_b, "pipe", [(i, (i + 1) % len(pipe)) for i in pipe])
-    xm = lax.ppermute(xb, "pipe", [(i, last - i) for i in pipe])
-    cm = lax.ppermute(sent_b, "pipe", [(i, (last - 1 - i) % len(pipe)) for i in pipe])
-
-    xga, xgb, lat = call(
+    half = len(pipe) // 2
+
+    def flip_x(value):
+        return lax.ppermute(value, "pipe", [(i, i ^ half) for i in pipe])
+
+    def turn_x(value):
+        return lax.ppermute(value, "pipe", [(i, i ^ (half - 1)) for i in pipe])
+
+    def flip_c(value):
+        return lax.ppermute(value, "pipe", [(i, i if i % half == half - 1 else i ^ half) for i in pipe])
+
+    def turn_c(value):
+        pairs = [(i, i - i % half + (half - 2 - i % half) % half) for i in pipe]
+        return lax.ppermute(value, "pipe", pairs)
+
+    cb = lax.ppermute(sent_b, "pipe", [(i - 1, i) for i in pipe if i % half != 0])
+    def end_flip(value):
+        return lax.ppermute(value, "pipe", [(i, i ^ half) for i in pipe if i % half == half - 1])
+
+    ca = lax.ppermute(sent_a, "pipe", [(i + 1, i) for i in pipe if i % half != half - 1])
+    xm = flip_x(xb)
+
+    far_a = lax.ppermute(sent_a, "pipe", [(i, i + half - 1) for i in pipe if i % half == 0])
+    xga, lat = call(
         latent_kernel,
-        [((TOKENS, WIDTH), BF16), ((TOKENS, WIDTH), BF16), ((PADDED, 2 * UNITS + 128), F32)],
+        [((TOKENS, WIDTH), BF16), ((PADDED, 2 * UNITS + 128), F32)],
         flops=2 * 2 * TOKENS * WIDTH * UNITS,
         name="latent",
     )(xa, xb, gain, wc)
+    lat, ca, far = lax.optimization_barrier((lat, ca, sent_b))
+    cm = turn_c(far)
     keep, send = call(
         code_kernel,
         [((HALF, SUM_COLS), F32), ((HALF, SUM_COLS), BF16)],
         [((PADDED, 2 * UNITS), F32)],
         flops=2 * 2 * TOKENS * WIDTH * UNITS,
         name="code",
-    )(ca, cb, we, lat)
+    )(ca, cb, sent_a, sent_b, we, lat)
+    recv = swap(send, 1)
+    recv, far_a = lax.optimization_barrier((recv, far_a))
     own, *parts = call(
         scatter_kernel,
         [((PART, SUM_COLS), F32)] + [((PART, SUM_COLS), BF16)] * 3,
         [((HALF, SUM_COLS), F32)],
         name="scatter",
-    )(keep, swap(send, 1))
+    )(keep, recv)
     parts = [swap(part, 2 * d) for d, part in zip((1, 2, 3), parts)]
-    out, mir = call(
-        latent_step_kernel,
-        [((PART, OWN_COLS), BF16), ((PART, MIR_COLS), BF16)],
-        name="step",
-    )(own, *parts, latent_gain)
+    total, mir = call(
+        sum_kernel,
+        [((PART, SUM_COLS), F32), ((PART, OWN_COLS), BF16)],
+        name="sum",
+    )(own, *parts)
+    mir, xm, cm, end_b = lax.optimization_barrier((mir, xm, cm, sent_b))
+    far_b = end_flip(end_b)
+    xm = turn_x(xm)
+    cm = flip_c(cm)
     mir = lax.ppermute(mir, "pipe", [(i, last - i) for i in pipe])
-    out = jnp.concatenate([out, mir], 1)
+    (out,) = call(latent_step_kernel, [((PART, ALL_COLS), BF16)], name="step")(
+        total, mir, latent_gain
+    )
+    out, xm, cm = lax.optimization_barrier((out, xm, cm))
+    far_b = lax.ppermute(far_b, "pipe", [(i, i - half + 1) for i in pipe if i % half == half - 1])
+    far_a = end_flip(far_a)
     (mine,) = call(gather_kernel, [((HALF, ALL_COLS), BF16)], name="gather")(
         out, *(swap(out, 2 * d) for d in (1, 2, 3))
     )
@@ -218,7 +282,7 @@
             [((PADDED, ALL_COLS), BF16)],
             flops=6 * 2 * TOKENS * WIDTH * UNITS,
             name="finish",
-        )(mine, other, ca, cb, xa, xb, xga, xm, cm, gain, wc)
+        )(mine, other, ca, cb, far_a, far_b, xa, xb, xga, xm, cm, gain, wc)
     )
 
 

time: 143 us -> 111 us (0.78)
  the two profiles are of different devices: /device:TPU:1 before, /device:TPU:126 now
where the time goes in v3:
time: 111 us; the launch traced here: 110 us
  starting transfers between devices  65.8 us (59%)
  waiting for transfers between devices  34.5 us (31%)
  Pallas kernels  4.37 us (4%)
  local copies, waits for them, and re-layouts  4.35 us (4%)
    ppermute x8, starting transfers between devices, swap(): return lax.ppermute(value, 'tensor', [(i, i ^ d) for i in tensor])  22.8 us
    ppermute x2, waiting for transfers between devices, end_flip(): lax.ppermute(value, 'pipe', [(i, i ^ half) for i in pipe if i % half == h...  15.2 us
    ppermute x1, waiting for transfers between devices, shards(): mir = lax.ppermute(mir, 'pipe', [(i, last - i) for i in pipe])  12.9 us
    ppermute x1, starting transfers between devices, flip_x(): return lax.ppermute(value, 'pipe', [(i, i ^ half) for i in pipe])  10 us
    ppermute x1, starting transfers between devices, turn_x(): return lax.ppermute(value, 'pipe', [(i, i ^ half - 1) for i in pipe])  9.91 us
    ppermute x2, starting transfers between devices, end_flip(): lax.ppermute(value, 'pipe', [(i, i ^ half) for i in pipe if i % half == h...  9.09 us
    ppermute x8, waiting for transfers between devices, swap(): return lax.ppermute(value, 'tensor', [(i, i ^ d) for i in tensor])  6.45 us
    ppermute x1, starting transfers between devices, shards(): mir = lax.ppermute(mir, 'pipe', [(i, last - i) for i in pipe])  4.48 us
  transfers between devices with their start and end apart: 19, of which 7 were waited for; matrix products, arithmetic and copies ran while one was open for 0% of the time, Pallas kernels for 2%

profile of v3, /device:TPU:126, one launch (start us, length us, event | category | flops | bytes accessed | tf_op | source)
XLA Modules:
  0.0 110.0 jit_solution(10289906742740786131)
XLA Ops:
  0.6 3.3 %collective-permute-start = (bf16[1,224,896]{2,1,0:T(8,128)(2,1)}, bf16[1,224,896]{2,1,0:T(8,128)(2,1)S(1)}, u32[]{:S(2)}, u32[]{:S(2)}) collective-permute-start(bf16[1,224,896]{2,1,0:T(8,128)(2,1)} %sa_ref.1), channel_id=1, source_target_pairs={{8,0},{16,8},{24,16},{32,24},{40,32},{48,40},{56,48},{64,56},{72,6... | collective-permute-start | bytes 1204232 | tf_op jit(solution)/shard_map/ppermute | solution.py:228
  3.9 1.3 %collective-permute-start.1 = (bf16[1,224,896]{2,1,0:T(8,128)(2,1)}, bf16[1,224,896]{2,1,0:T(8,128)(2,1)S(1)}, u32[]{:S(2)}, u32[]{:S(2)}) collective-permute-start(bf16[1,224,896]{2,1,0:T(8,128)(2,1)} %sb_ref.1), channel_id=1, source_target_pairs={{0,8},{8,16},{16,24},{24,32},{32,40},{40,48},{48,56},{56,64},{64,7... | collective-permute-start | bytes 1204232 | tf_op jit(solution)/shard_map/ppermute | solution.py:224
  5.2 1.3 %collective-permute-start.3 = (bf16[1,224,896]{2,1,0:T(8,128)(2,1)}, bf16[1,224,896]{2,1,0:T(8,128)(2,1)S(1)}, u32[]{:S(2)}, u32[]{:S(2)}) collective-permute-start(bf16[1,224,896]{2,1,0:T(8,128)(2,1)} %sa_ref.1), channel_id=1, source_target_pairs={{0,248},{256,504},{1,249},{257,505},{2,250},{258,506},{3,251},{259... | collective-permute-start | bytes 1204232 | tf_op jit(solution)/shard_map/ppermute | solution.py:231
  6.5 10.0 %collective-permute-start.7 = (bf16[1,224,896]{2,1,0:T(8,128)(2,1)}, bf16[1,224,896]{2,1,0:T(8,128)(2,1)S(1)}, u32[]{:S(2)}, u32[]{:S(2)}) collective-permute-start(bf16[1,224,896]{2,1,0:T(8,128)(2,1)} %xb_ref.3), channel_id=1, source_target_pairs={{0,256},{8,264},{16,272},{24,280},{32,288},{40,296},{48,304},{56,3... | collective-permute-start | bytes 1204232 | tf_op jit(solution)/shard_map/ppermute | solution.py:212
  16.5 0.0 copy-start
  16.6 1.2 %copy-done = bf16[1,2,256,896]{3,2,1,0:T(8,128)(2,1)S(1)} copy-done((bf16[1,2,256,896]{3,2,1,0:T(8,128)(2,1)S(1)}, bf16[1,2,256,896]{3,2,1,0:T(8,128)(2,1)}, u32[]{:S(2)}) %copy-start) | copy-done | bytes 917528
  17.7 1.0 copy-done.2
  18.7 1.0 copy-done.4
  19.7 0.7 copy-done.9
  20.4 0.5 latent.1
  21.0 0.0 collective-permute-done.ca_ref
  21.0 0.4 copy-done.8
  21.4 0.7 collective-permute-start.8
  22.1 0.6 code.1
  22.7 1.9 %collective-permute-start.2 = (bf16[128,1152]{1,0:T(8,128)(2,1)S(1)}, bf16[128,1152]{1,0:T(8,128)(2,1)S(1)}, u32[]{:S(2)}, u32[]{:S(2)}) collective-permute-start(bf16[128,1152]{1,0:T(8,128)(2,1)S(1)} %get-tuple-element.30), channel_id=1, source_target_pairs={{0,1},{1,0},{2,3},{3,2},{4,5},{5,4},{6,7},{7,6},{8,9},{9,8},{10,11... | collective-permute-start | bytes 884744 | tf_op jit(solution)/shard_map/ppermute | solution.py:207
  24.6 0.0 collective-permute-done.3
  24.6 1.5 %collective-permute-done.2.recv_ref = bf16[128,1152]{1,0:T(8,128)(2,1)S(1)} collective-permute-done((bf16[128,1152]{1,0:T(8,128)(2,1)S(1)}, bf16[128,1152]{1,0:T(8,128)(2,1)S(1)}, u32[]{:S(2)}, u32[]{:S(2)}) %collective-permute-start.2) | collective-permute-done | bytes 294944 | tf_op jit(solution)/shard_map/ppermute | solution.py:207
  26.2 0.3 scatter.1
  26.4 0.0 copy-start.1
  26.4 2.6 %collective-permute-start.4 = (bf16[32,1152]{1,0:T(8,128)(2,1)S(1)}, bf16[32,1152]{1,0:T(8,128)(2,1)S(1)}, u32[]{:S(2)}, u32[]{:S(2)}) collective-permute-start(bf16[32,1152]{1,0:T(8,128)(2,1)S(1)} %get-tuple-element.33), channel_id=1, source_target_pairs={{0,2},{1,3},{2,0},{3,1},{4,6},{5,7},{6,4},{7,5},{8,10},{9,11},{10,... | collective-permute-start | bytes 221192 | tf_op jit(solution)/shard_map/ppermute | solution.py:207
  29.1 4.3 %collective-permute-start.5 = (bf16[32,1152]{1,0:T(8,128)(2,1)S(1)}, bf16[32,1152]{1,0:T(8,128)(2,1)S(1)}, u32[]{:S(2)}, u32[]{:S(2)}) collective-permute-start(bf16[32,1152]{1,0:T(8,128)(2,1)S(1)} %get-tuple-element.34), channel_id=1, source_target_pairs={{0,4},{1,5},{2,6},{3,7},{4,0},{5,1},{6,2},{7,3},{8,12},{9,13},{10,... | collective-permute-start | bytes 221192 | tf_op jit(solution)/shard_map/ppermute | solution.py:207
  33.4 2.5 %collective-permute-start.6 = (bf16[32,1152]{1,0:T(8,128)(2,1)S(1)}, bf16[32,1152]{1,0:T(8,128)(2,1)S(1)}, u32[]{:S(2)}, u32[]{:S(2)}) collective-permute-start(bf16[32,1152]{1,0:T(8,128)(2,1)S(1)} %get-tuple-element.35), channel_id=1, source_target_pairs={{0,6},{1,7},{2,4},{3,5},{4,2},{5,3},{6,0},{7,1},{8,14},{9,15},{10,... | collective-permute-start | bytes 221192 | tf_op jit(solution)/shard_map/ppermute | solution.py:207
  35.8 0.7 collective-permute-done.4.one_ref
  36.5 1.3 %collective-permute-done.5.two_ref = bf16[32,1152]{1,0:T(8,128)(2,1)S(1)} collective-permute-done((bf16[32,1152]{1,0:T(8,128)(2,1)S(1)}, bf16[32,1152]{1,0:T(8,128)(2,1)S(1)}, u32[]{:S(2)}, u32[]{:S(2)}) %collective-permute-start.5) | collective-permute-done | bytes 73760 | tf_op jit(solution)/shard_map/ppermute | solution.py:207
  37.8 2.6 %collective-permute-done.6.three_ref = bf16[32,1152]{1,0:T(8,128)(2,1)S(1)} collective-permute-done((bf16[32,1152]{1,0:T(8,128)(2,1)S(1)}, bf16[32,1152]{1,0:T(8,128)(2,1)S(1)}, u32[]{:S(2)}, u32[]{:S(2)}) %collective-permute-start.6) | collective-permute-done | bytes 73760 | tf_op jit(solution)/shard_map/ppermute | solution.py:207
  40.4 0.2 sum.1
  40.6 0.0 collective-permute-done.7
  40.6 9.9 %collective-permute-start.10 = (bf16[1,224,896]{2,1,0:T(8,128)(2,1)S(1)}, bf16[1,224,896]{2,1,0:T(8,128)(2,1)S(1)}, u32[]{:S(2)}, u32[]{:S(2)}) collective-permute-start(bf16[1,224,896]{2,1,0:T(8,128)(2,1)S(1)} %collective-permute-done.7), channel_id=1, source_target_pairs={{0,248},{8,240},{16,232},{24,224},{32,216},{40,208},{48,200},{56,1... | collective-permute-start | bytes 1204232 | tf_op jit(solution)/shard_map/ppermute | solution.py:215
  50.5 0.7 collective-permute-start.11
  51.2 4.7 %collective-permute-start.17 = (bf16[1,224,896]{2,1,0:T(8,128)(2,1)S(1)}, bf16[1,224,896]{2,1,0:T(8,128)(2,1)S(1)}, u32[]{:S(2)}, u32[]{:S(2)}) collective-permute-start(bf16[1,224,896]{2,1,0:T(8,128)(2,1)S(1)} %copy-done.8), channel_id=1, source_target_pairs={{248,504},{504,248},{249,505},{505,249},{250,506},{506,250},{251,5... | collective-permute-start | bytes 1204232 | tf_op jit(solution)/shard_map/ppermute | solution.py:226
  56.0 4.5 %collective-permute-start.9 = (bf16[32,896]{1,0:T(8,128)(2,1)S(1)}, bf16[32,896]{1,0:T(8,128)(2,1)S(1)}, u32[]{:S(2)}, u32[]{:S(2)}) collective-permute-start(bf16[32,896]{1,0:T(8,128)(2,1)S(1)} %get-tuple-element.39), channel_id=1, source_target_pairs={{0,504},{8,496},{16,488},{24,480},{32,472},{40,464},{48,456},{56,4... | collective-permute-start | bytes 172040 | tf_op jit(solution)/shard_map/ppermute | solution.py:265
  60.4 12.9 %collective-permute-done.9.far_ref = bf16[32,896]{1,0:T(8,128)(2,1)S(1)} collective-permute-done((bf16[32,896]{1,0:T(8,128)(2,1)S(1)}, bf16[32,896]{1,0:T(8,128)(2,1)S(1)}, u32[]{:S(2)}, u32[]{:S(2)}) %collective-permute-start.9) | collective-permute-done | bytes 57376 | tf_op jit(solution)/shard_map/ppermute | solution.py:265
  73.3 0.5 step.1.own_ref
  73.8 0.0 copy-start.3
  73.9 0.0 copy-start.10
  73.9 0.0 collective-permute-done.11.cm_ref
  73.9 4.3 %collective-permute-start.14 = (bf16[32,1408]{1,0:T(8,128)(2,1)S(1)}, bf16[32,1408]{1,0:T(8,128)(2,1)S(1)}, u32[]{:S(2)}, u32[]{:S(2)}) collective-permute-start(bf16[32,1408]{1,0:T(8,128)(2,1)S(1)} %step.1.own_ref), channel_id=1, source_target_pairs={{0,6},{1,7},{2,4},{3,5},{4,2},{5,3},{6,0},{7,1},{8,14},{9,15},{10,... | collective-permute-start | bytes 270344 | tf_op jit(solution)/shard_map/ppermute | solution.py:207
  78.2 1.9 %collective-permute-start.13 = (bf16[32,1408]{1,0:T(8,128)(2,1)S(1)}, bf16[32,1408]{1,0:T(8,128)(2,1)S(1)}, u32[]{:S(2)}, u32[]{:S(2)}) collective-permute-start(bf16[32,1408]{1,0:T(8,128)(2,1)S(1)} %step.1.own_ref), channel_id=1, source_target_pairs={{0,4},{1,5},{2,6},{3,7},{4,0},{5,1},{6,2},{7,3},{8,12},{9,13},{10,... | collective-permute-start | bytes 270344 | tf_op jit(solution)/shard_map/ppermute | solution.py:207
  80.1 3.4 %collective-permute-start.12 = (bf16[32,1408]{1,0:T(8,128)(2,1)S(1)}, bf16[32,1408]{1,0:T(8,128)(2,1)S(1)}, u32[]{:S(2)}, u32[]{:S(2)}) collective-permute-start(bf16[32,1408]{1,0:T(8,128)(2,1)S(1)} %step.1.own_ref), channel_id=1, source_target_pairs={{0,2},{1,3},{2,0},{3,1},{4,6},{5,7},{6,4},{7,5},{8,10},{9,11},{10,... | collective-permute-start | bytes 270344 | tf_op jit(solution)/shard_map/ppermute | solution.py:207
  83.5 4.4 %collective-permute-start.16 = (bf16[1,224,896]{2,1,0:T(8,128)(2,1)S(1)}, bf16[1,224,896]{2,1,0:T(8,128)(2,1)S(1)}, u32[]{:S(2)}, u32[]{:S(2)}) collective-permute-start(bf16[1,224,896]{2,1,0:T(8,128)(2,1)S(1)} %collective-permute-done.3), channel_id=1, source_target_pairs={{248,504},{504,248},{249,505},{505,249},{250,506},{506,250},{251,5... | collective-permute-start | bytes 1204232 | tf_op jit(solution)/shard_map/ppermute | solution.py:226
  87.9 0.0 collective-permute-done.17
  87.9 2.3 %collective-permute-start.18 = (bf16[1,224,896]{2,1,0:T(8,128)(2,1)S(1)}, bf16[1,224,896]{2,1,0:T(8,128)(2,1)S(1)}, u32[]{:S(2)}, u32[]{:S(2)}) collective-permute-start(bf16[1,224,896]{2,1,0:T(8,128)(2,1)S(1)} %collective-permute-done.17), channel_id=1, source_target_pairs={{248,0},{504,256},{249,1},{505,257},{250,2},{506,258},{251,3},{507... | collective-permute-start | bytes 1204232 | tf_op jit(solution)/shard_map/ppermute | solution.py:270
  90.2 0.0 collective-permute-done.14.three_ref
  90.2 0.3 collective-permute-done.13.two_ref
  90.5 0.0 collective-permute-done.12.one_ref
  90.5 1.9 %collective-permute-start.15 = (bf16[128,1408]{1,0:T(8,128)(2,1)S(1)}, bf16[128,1408]{1,0:T(8,128)(2,1)S(1)}, u32[]{:S(2)}, u32[]{:S(2)}) collective-permute-start(bf16[128,1408]{1,0:T(8,128)(2,1)S(1)} %gather.1.mine_ref), channel_id=1, source_target_pairs={{0,1},{1,0},{2,3},{3,2},{4,5},{5,4},{6,7},{7,6},{8,9},{9,8},{10,11... | collective-permute-start | bytes 1081352 | tf_op jit(solution)/shard_map/ppermute | solution.py:207
  92.4 15.2 %collective-permute-done.16.far_a_ref = bf16[1,224,896]{2,1,0:T(8,128)(2,1)S(1)} collective-permute-done((bf16[1,224,896]{2,1,0:T(8,128)(2,1)S(1)}, bf16[1,224,896]{2,1,0:T(8,128)(2,1)S(1)}, u32[]{:S(2)}, u32[]{:S(2)}) %collective-permute-start.16) | collective-permute-done | bytes 401440 | tf_op jit(solution)/shard_map/ppermute | solution.py:226
  107.7 2.3 %finish.1 = (bf16[1,224,896]{2,1,0:T(8,128)(2,1)}, bf16[1,224,896]{2,1,0:T(8,128)(2,1)}, bf16[1,256,896]{2,1,0:T(8,128)(2,1)}, bf16[1,256,896]{2,1,0:T(8,128)(2,1)}) custom-call(bf16[128,1408]{1,0:T(8,128)(2,1)S(1)} %gather.1.mine_ref, bf16[128,1408]{1,0:T(8,128)(2,1)S(1)} %collective-permute-done.15.other_ref, ...), custom_call_target="tpu_custom_call" | custom-call | flops 616562688 | bytes 4194304 | tf_op jit(solution)/shard_map/finish/pallas_call | solution.py:279
  (21 shorter events, 0.1 us)
Async XLA Ops:
  0.6 20.3 %collective-permute-start = (bf16[1,224,896]{2,1,0:T(8,128)(2,1)}, bf16[1,224,896]{2,1,0:T(8,128)(2,1)S(1)}, u32[]{:S(2)}, u32[]{:S(2)}) collective-permute-start(bf16[1,224,896]{2,1,0:T(8,128)(2,1)} %sa_ref.1), channel_id=1, source_target_pairs={{8,0},{16,8},{24,16},{32,24},{40,32},{48,40},{56,48},{64,56},{72,6... | collective-permute-start | bytes 1204232 | tf_op jit(solution)/shard_map/ppermute | solution.py:228
  3.9 18.2 %collective-permute-start.1 = (bf16[1,224,896]{2,1,0:T(8,128)(2,1)}, bf16[1,224,896]{2,1,0:T(8,128)(2,1)S(1)}, u32[]{:S(2)}, u32[]{:S(2)}) collective-permute-start(bf16[1,224,896]{2,1,0:T(8,128)(2,1)} %sb_ref.1), channel_id=1, source_target_pairs={{0,8},{8,16},{16,24},{24,32},{32,40},{40,48},{48,56},{56,64},{64,7... | collective-permute-start | bytes 1204232 | tf_op jit(solution)/shard_map/ppermute | solution.py:224
  5.2 19.4 %collective-permute-start.3 = (bf16[1,224,896]{2,1,0:T(8,128)(2,1)}, bf16[1,224,896]{2,1,0:T(8,128)(2,1)S(1)}, u32[]{:S(2)}, u32[]{:S(2)}) collective-permute-start(bf16[1,224,896]{2,1,0:T(8,128)(2,1)} %sa_ref.1), channel_id=1, source_target_pairs={{0,248},{256,504},{1,249},{257,505},{2,250},{258,506},{3,251},{259... | collective-permute-start | bytes 1204232 | tf_op jit(solution)/shard_map/ppermute | solution.py:231
  6.5 34.1 %collective-permute-start.7 = (bf16[1,224,896]{2,1,0:T(8,128)(2,1)}, bf16[1,224,896]{2,1,0:T(8,128)(2,1)S(1)}, u32[]{:S(2)}, u32[]{:S(2)}) collective-permute-start(bf16[1,224,896]{2,1,0:T(8,128)(2,1)} %xb_ref.3), channel_id=1, source_target_pairs={{0,256},{8,264},{16,272},{24,280},{32,288},{40,296},{48,304},{56,3... | collective-permute-start | bytes 1204232 | tf_op jit(solution)/shard_map/ppermute | solution.py:212
  16.5 1.2 %copy-start = (bf16[1,2,256,896]{3,2,1,0:T(8,128)(2,1)S(1)}, bf16[1,2,256,896]{3,2,1,0:T(8,128)(2,1)}, u32[]{:S(2)}) copy-start(bf16[1,2,256,896]{3,2,1,0:T(8,128)(2,1)} %wc_ref.3) | copy-start | bytes 2752516
  17.7 1.0 copy-start.2
  18.7 1.0 copy-start.4
  19.7 0.7 copy-start.9
  20.4 1.0 copy-start.8
  20.4 1.7 %copy-start.6 = (bf16[1,2,256,896]{3,2,1,0:T(8,128)(2,1)S(1)}, bf16[1,2,256,896]{3,2,1,0:T(8,128)(2,1)}, u32[]{:S(2)}) copy-start(bf16[1,2,256,896]{3,2,1,0:T(8,128)(2,1)} %we_ref.1) | copy-start | bytes 2752516
  20.4 1.7 %copy-start.7 = (bf16[1,224,896]{2,1,0:T(8,128)(2,1)S(1)}, bf16[1,224,896]{2,1,0:T(8,128)(2,1)}, u32[]{:S(2)}) copy-start(bf16[1,224,896]{2,1,0:T(8,128)(2,1)} %sa_ref.1) | copy-start | bytes 1204228
  21.4 19.2 %collective-permute-start.8 = (bf16[1,224,896]{2,1,0:T(8,128)(2,1)S(1)}, bf16[1,224,896]{2,1,0:T(8,128)(2,1)S(1)}, u32[]{:S(2)}, u32[]{:S(2)}) collective-permute-start(bf16[1,224,896]{2,1,0:T(8,128)(2,1)S(1)} %copy-done.8), channel_id=1, source_target_pairs={{0,240},{8,232},{16,224},{24,216},{32,208},{40,200},{48,192},{56,1... | collective-permute-start | bytes 1204232 | tf_op jit(solution)/shard_map/ppermute | solution.py:222
  22.7 3.5 %collective-permute-start.2 = (bf16[128,1152]{1,0:T(8,128)(2,1)S(1)}, bf16[128,1152]{1,0:T(8,128)(2,1)S(1)}, u32[]{:S(2)}, u32[]{:S(2)}) collective-permute-start(bf16[128,1152]{1,0:T(8,128)(2,1)S(1)} %get-tuple-element.30), channel_id=1, source_target_pairs={{0,1},{1,0},{2,3},{3,2},{4,5},{5,4},{6,7},{7,6},{8,9},{9,8},{10,11... | collective-permute-start | bytes 884744 | tf_op jit(solution)/shard_map/ppermute | solution.py:207
  26.2 47.2 %copy-start.11 = (f32[1,2,256]{2,1,0:T(2,128)S(1)}, f32[1,2,256]{2,1,0:T(2,128)}, u32[]{:S(2)}) copy-start(f32[1,2,256]{2,1,0:T(2,128)} %gain_ref.4) | copy-start | bytes 6148
  26.2 81.5 %copy-start.5 = (bf16[1,224,896]{2,1,0:T(8,128)(2,1)S(1)}, bf16[1,224,896]{2,1,0:T(8,128)(2,1)}, u32[]{:S(2)}) copy-start(bf16[1,224,896]{2,1,0:T(8,128)(2,1)} %xb_ref.3) | copy-start | bytes 1204228
  26.4 81.2 %copy-start.1 = (bf16[1,2,256,896]{3,2,1,0:T(8,128)(2,1)S(1)}, bf16[1,2,256,896]{3,2,1,0:T(8,128)(2,1)}, u32[]{:S(2)}) copy-start(bf16[1,2,256,896]{3,2,1,0:T(8,128)(2,1)} %wc_ref.3) | copy-start | bytes 2752516
  26.4 10.1 %collective-permute-start.4 = (bf16[32,1152]{1,0:T(8,128)(2,1)S(1)}, bf16[32,1152]{1,0:T(8,128)(2,1)S(1)}, u32[]{:S(2)}, u32[]{:S(2)}) collective-permute-start(bf16[32,1152]{1,0:T(8,128)(2,1)S(1)} %get-tuple-element.33), channel_id=1, source_target_pairs={{0,2},{1,3},{2,0},{3,1},{4,6},{5,7},{6,4},{7,5},{8,10},{9,11},{10,... | collective-permute-start | bytes 221192 | tf_op jit(solution)/shard_map/ppermute | solution.py:207
  29.1 8.8 %collective-permute-start.5 = (bf16[32,1152]{1,0:T(8,128)(2,1)S(1)}, bf16[32,1152]{1,0:T(8,128)(2,1)S(1)}, u32[]{:S(2)}, u32[]{:S(2)}) collective-permute-start(bf16[32,1152]{1,0:T(8,128)(2,1)S(1)} %get-tuple-element.34), channel_id=1, source_target_pairs={{0,4},{1,5},{2,6},{3,7},{4,0},{5,1},{6,2},{7,3},{8,12},{9,13},{10,... | collective-permute-start | bytes 221192 | tf_op jit(solution)/shard_map/ppermute | solution.py:207
  33.4 7.1 %collective-permute-start.6 = (bf16[32,1152]{1,0:T(8,128)(2,1)S(1)}, bf16[32,1152]{1,0:T(8,128)(2,1)S(1)}, u32[]{:S(2)}, u32[]{:S(2)}) collective-permute-start(bf16[32,1152]{1,0:T(8,128)(2,1)S(1)} %get-tuple-element.35), channel_id=1, source_target_pairs={{0,6},{1,7},{2,4},{3,5},{4,2},{5,3},{6,0},{7,1},{8,14},{9,15},{10,... | collective-permute-start | bytes 221192 | tf_op jit(solution)/shard_map/ppermute | solution.py:207
  40.6 33.3 %collective-permute-start.10 = (bf16[1,224,896]{2,1,0:T(8,128)(2,1)S(1)}, bf16[1,224,896]{2,1,0:T(8,128)(2,1)S(1)}, u32[]{:S(2)}, u32[]{:S(2)}) collective-permute-start(bf16[1,224,896]{2,1,0:T(8,128)(2,1)S(1)} %collective-permute-done.7), channel_id=1, source_target_pairs={{0,248},{8,240},{16,232},{24,224},{32,216},{40,208},{48,200},{56,1... | collective-permute-start | bytes 1204232 | tf_op jit(solution)/shard_map/ppermute | solution.py:215
  50.5 23.4 %collective-permute-start.11 = (bf16[1,224,896]{2,1,0:T(8,128)(2,1)S(1)}, bf16[1,224,896]{2,1,0:T(8,128)(2,1)S(1)}, u32[]{:S(2)}, u32[]{:S(2)}) collective-permute-start(bf16[1,224,896]{2,1,0:T(8,128)(2,1)S(1)} %collective-permute-done.8), channel_id=1, source_target_pairs={{0,256},{8,264},{16,272},{24,280},{32,288},{40,296},{48,304},{56,3... | collective-permute-start | bytes 1204232 | tf_op jit(solution)/shard_map/ppermute | solution.py:218
  51.2 36.6 %collective-permute-start.17 = (bf16[1,224,896]{2,1,0:T(8,128)(2,1)S(1)}, bf16[1,224,896]{2,1,0:T(8,128)(2,1)S(1)}, u32[]{:S(2)}, u32[]{:S(2)}) collective-permute-start(bf16[1,224,896]{2,1,0:T(8,128)(2,1)S(1)} %copy-done.8), channel_id=1, source_target_pairs={{248,504},{504,248},{249,505},{505,249},{250,506},{506,250},{251,5... | collective-permute-start | bytes 1204232 | tf_op jit(solution)/shard_map/ppermute | solution.py:226
  56.0 17.4 %collective-permute-start.9 = (bf16[32,896]{1,0:T(8,128)(2,1)S(1)}, bf16[32,896]{1,0:T(8,128)(2,1)S(1)}, u32[]{:S(2)}, u32[]{:S(2)}) collective-permute-start(bf16[32,896]{1,0:T(8,128)(2,1)S(1)} %get-tuple-element.39), channel_id=1, source_target_pairs={{0,504},{8,496},{16,488},{24,480},{32,472},{40,464},{48,456},{56,4... | collective-permute-start | bytes 172040 | tf_op jit(solution)/shard_map/ppermute | solution.py:265
  73.8 33.8 %copy-start.3 = (bf16[1,224,896]{2,1,0:T(8,128)(2,1)S(1)}, bf16[1,224,896]{2,1,0:T(8,128)(2,1)}, u32[]{:S(2)}) copy-start(bf16[1,224,896]{2,1,0:T(8,128)(2,1)} %xa_ref.3) | copy-start | bytes 1204228
  73.9 33.8 %copy-start.10 = (f32[1,2,896]{2,1,0:T(2,128)S(1)}, f32[1,2,896]{2,1,0:T(2,128)}, u32[]{:S(2)}) copy-start(f32[1,2,896]{2,1,0:T(2,128)} %gain_ref.5) | copy-start | bytes 21508
  73.9 16.3 %collective-permute-start.14 = (bf16[32,1408]{1,0:T(8,128)(2,1)S(1)}, bf16[32,1408]{1,0:T(8,128)(2,1)S(1)}, u32[]{:S(2)}, u32[]{:S(2)}) collective-permute-start(bf16[32,1408]{1,0:T(8,128)(2,1)S(1)} %step.1.own_ref), channel_id=1, source_target_pairs={{0,6},{1,7},{2,4},{3,5},{4,2},{5,3},{6,0},{7,1},{8,14},{9,15},{10,... | collective-permute-start | bytes 270344 | tf_op jit(solution)/shard_map/ppermute | solution.py:207
  78.2 12.3 %collective-permute-start.13 = (bf16[32,1408]{1,0:T(8,128)(2,1)S(1)}, bf16[32,1408]{1,0:T(8,128)(2,1)S(1)}, u32[]{:S(2)}, u32[]{:S(2)}) collective-permute-start(bf16[32,1408]{1,0:T(8,128)(2,1)S(1)} %step.1.own_ref), channel_id=1, source_target_pairs={{0,4},{1,5},{2,6},{3,7},{4,0},{5,1},{6,2},{7,3},{8,12},{9,13},{10,... | collective-permute-start | bytes 270344 | tf_op jit(solution)/shard_map/ppermute | solution.py:207
  80.1 10.4 %collective-permute-start.12 = (bf16[32,1408]{1,0:T(8,128)(2,1)S(1)}, bf16[32,1408]{1,0:T(8,128)(2,1)S(1)}, u32[]{:S(2)}, u32[]{:S(2)}) collective-permute-start(bf16[32,1408]{1,0:T(8,128)(2,1)S(1)} %step.1.own_ref), channel_id=1, source_target_pairs={{0,2},{1,3},{2,0},{3,1},{4,6},{5,7},{6,4},{7,5},{8,10},{9,11},{10,... | collective-permute-start | bytes 270344 | tf_op jit(solution)/shard_map/ppermute | solution.py:207
  83.5 24.1 %collective-permute-start.16 = (bf16[1,224,896]{2,1,0:T(8,128)(2,1)S(1)}, bf16[1,224,896]{2,1,0:T(8,128)(2,1)S(1)}, u32[]{:S(2)}, u32[]{:S(2)}) collective-permute-start(bf16[1,224,896]{2,1,0:T(8,128)(2,1)S(1)} %collective-permute-done.3), channel_id=1, source_target_pairs={{248,504},{504,248},{249,505},{505,249},{250,506},{506,250},{251,5... | collective-permute-start | bytes 1204232 | tf_op jit(solution)/shard_map/ppermute | solution.py:226
  87.9 19.7 %collective-permute-start.18 = (bf16[1,224,896]{2,1,0:T(8,128)(2,1)S(1)}, bf16[1,224,896]{2,1,0:T(8,128)(2,1)S(1)}, u32[]{:S(2)}, u32[]{:S(2)}) collective-permute-start(bf16[1,224,896]{2,1,0:T(8,128)(2,1)S(1)} %collective-permute-done.17), channel_id=1, source_target_pairs={{248,0},{504,256},{249,1},{505,257},{250,2},{506,258},{251,3},{507... | collective-permute-start | bytes 1204232 | tf_op jit(solution)/shard_map/ppermute | solution.py:270
  90.5 17.1 %collective-permute-start.15 = (bf16[128,1408]{1,0:T(8,128)(2,1)S(1)}, bf16[128,1408]{1,0:T(8,128)(2,1)S(1)}, u32[]{:S(2)}, u32[]{:S(2)}) collective-permute-start(bf16[128,1408]{1,0:T(8,128)(2,1)S(1)} %gather.1.mine_ref), channel_id=1, source_target_pairs={{0,1},{1,0},{2,3},{3,2},{4,5},{5,4},{6,7},{7,6},{8,9},{9,8},{10,11... | collective-permute-start | bytes 1081352 | tf_op jit(solution)/shard_map/ppermute | solution.py:207

commit v4 on v3

--- a/solution.py
+++ b/solution.py
@@ -50,10 +50,14 @@
     squares = []
     for s, x_ref in enumerate((xa_ref, xb_ref)):
         x = x_ref[0].astype(F32)
-        xg = (x * gain_ref[0, s : s + 1, :]).astype(BF16)
+        scaled = x * gain_ref[0, s : s + 1, :]
+        xg = scaled.astype(BF16)
+        rest = (scaled - xg.astype(F32)).astype(BF16)
         if s == 0:
             xga_ref[...] = xg
-        lat_ref[0:TOKENS, s * UNITS : (s + 1) * UNITS] = contract_last(xg, wc_ref[0, s])
+        lat_ref[0:TOKENS, s * UNITS : (s + 1) * UNITS] = contract_last(
+            xg, wc_ref[0, s]
+        ) + contract_last(rest, wc_ref[0, s])
         squares.append(jnp.sum(x * x, -1, keepdims=True))
     lane = lanes(TOKENS)
     block = jnp.where(lane == 0, squares[0], jnp.where(lane == 1, squares[1], 0.0))
@@ -266,12 +270,13 @@
     (out,) = call(latent_step_kernel, [((PART, ALL_COLS), BF16)], name="step")(
         total, mir, latent_gain
     )
-    out, xm, cm = lax.optimization_barrier((out, xm, cm))
+    out, xm = lax.optimization_barrier((out, xm))
     far_b = lax.ppermute(far_b, "pipe", [(i, i - half + 1) for i in pipe if i % half == half - 1])
     far_a = end_flip(far_a)
     (mine,) = call(gather_kernel, [((HALF, ALL_COLS), BF16)], name="gather")(
         out, *(swap(out, 2 * d) for d in (1, 2, 3))
     )
+    mine, cm = lax.optimization_barrier((mine, cm))
     other = swap(mine, 1)
     big = ((1, TOKENS, WIDTH), BF16)
     grad = ((1, UNITS, WIDTH), BF16)

time: 111 us -> 111 us (level)
  transfers between devices with their start and end apart: 19 -> 19, of which waited for: 7 -> 6; matrix products, arithmetic and copies ran while one was open for 0% -> 0% of each run, Pallas kernels for 2% -> 2%
where the time goes in v4:
time: 111 us; the launch traced here: 110 us
  starting transfers between devices  65.9 us (59%)
  waiting for transfers between devices  34.4 us (31%)
  Pallas kernels  4.64 us (4%)
  local copies, waits for them, and re-layouts  4.08 us (4%)
    ppermute x8, starting transfers between devices, swap(): return lax.ppermute(value, 'tensor', [(i, i ^ d) for i in tensor])  22.7 us
    ppermute x2, waiting for transfers between devices, end_flip(): lax.ppermute(value, 'pipe', [(i, i ^ half) for i in pipe if i % half == h...  15.3 us
    ppermute x1, waiting for transfers between devices, shards(): mir = lax.ppermute(mir, 'pipe', [(i, last - i) for i in pipe])  12.9 us
    ppermute x1, starting transfers between devices, flip_x(): return lax.ppermute(value, 'pipe', [(i, i ^ half) for i in pipe])  10 us
    ppermute x1, starting transfers between devices, turn_x(): return lax.ppermute(value, 'pipe', [(i, i ^ half - 1) for i in pipe])  9.91 us
    ppermute x2, starting transfers between devices, end_flip(): lax.ppermute(value, 'pipe', [(i, i ^ half) for i in pipe if i % half == h...  9 us
    ppermute x8, waiting for transfers between devices, swap(): return lax.ppermute(value, 'tensor', [(i, i ^ d) for i in tensor])  6.16 us
    ppermute x1, starting transfers between devices, shards(): mir = lax.ppermute(mir, 'pipe', [(i, last - i) for i in pipe])  4.48 us
  transfers between devices with their start and end apart: 19, of which 6 were waited for; matrix products, arithmetic and copies ran while one was open for 0% of the time, Pallas kernels for 2%

profile of v4, /device:TPU:126, one launch (start us, length us, event | category | flops | bytes accessed | tf_op | source)
XLA Modules:
  0.0 110.0 jit_solution(4504607271359981393)
XLA Ops:
  0.6 3.3 %collective-permute-start = (bf16[1,224,896]{2,1,0:T(8,128)(2,1)}, bf16[1,224,896]{2,1,0:T(8,128)(2,1)S(1)}, u32[]{:S(2)}, u32[]{:S(2)}) collective-permute-start(bf16[1,224,896]{2,1,0:T(8,128)(2,1)} %sa_ref.1), channel_id=1, source_target_pairs={{8,0},{16,8},{24,16},{32,24},{40,32},{48,40},{56,48},{64,56},{72,6... | collective-permute-start | bytes 1204232 | tf_op jit(solution)/shard_map/ppermute | solution.py:232
  3.9 1.3 %collective-permute-start.1 = (bf16[1,224,896]{2,1,0:T(8,128)(2,1)}, bf16[1,224,896]{2,1,0:T(8,128)(2,1)S(1)}, u32[]{:S(2)}, u32[]{:S(2)}) collective-permute-start(bf16[1,224,896]{2,1,0:T(8,128)(2,1)} %sb_ref.1), channel_id=1, source_target_pairs={{0,8},{8,16},{16,24},{24,32},{32,40},{40,48},{48,56},{56,64},{64,7... | collective-permute-start | bytes 1204232 | tf_op jit(solution)/shard_map/ppermute | solution.py:228
  5.2 1.3 %collective-permute-start.3 = (bf16[1,224,896]{2,1,0:T(8,128)(2,1)}, bf16[1,224,896]{2,1,0:T(8,128)(2,1)S(1)}, u32[]{:S(2)}, u32[]{:S(2)}) collective-permute-start(bf16[1,224,896]{2,1,0:T(8,128)(2,1)} %sa_ref.1), channel_id=1, source_target_pairs={{0,248},{256,504},{1,249},{257,505},{2,250},{258,506},{3,251},{259... | collective-permute-start | bytes 1204232 | tf_op jit(solution)/shard_map/ppermute | solution.py:235
  6.5 10.0 %collective-permute-start.7 = (bf16[1,224,896]{2,1,0:T(8,128)(2,1)}, bf16[1,224,896]{2,1,0:T(8,128)(2,1)S(1)}, u32[]{:S(2)}, u32[]{:S(2)}) collective-permute-start(bf16[1,224,896]{2,1,0:T(8,128)(2,1)} %xb_ref.3), channel_id=1, source_target_pairs={{0,256},{8,264},{16,272},{24,280},{32,288},{40,296},{48,304},{56,3... | collective-permute-start | bytes 1204232 | tf_op jit(solution)/shard_map/ppermute | solution.py:216
  16.5 0.0 copy-start
  16.6 1.2 %copy-done = bf16[1,2,256,896]{3,2,1,0:T(8,128)(2,1)S(1)} copy-done((bf16[1,2,256,896]{3,2,1,0:T(8,128)(2,1)S(1)}, bf16[1,2,256,896]{3,2,1,0:T(8,128)(2,1)}, u32[]{:S(2)}) %copy-start) | copy-done | bytes 917528
  17.7 1.0 copy-done.2
  18.7 1.0 copy-done.4
  19.7 0.7 copy-done.9
  20.4 0.8 latent.1
  21.2 0.0 collective-permute-done.ca_ref
  21.2 0.2 copy-done.8
  21.4 0.7 collective-permute-start.8
  22.1 0.0 collective-permute-done.1.cb_ref
  22.1 0.6 code.1
  22.7 1.9 %collective-permute-start.2 = (bf16[128,1152]{1,0:T(8,128)(2,1)S(1)}, bf16[128,1152]{1,0:T(8,128)(2,1)S(1)}, u32[]{:S(2)}, u32[]{:S(2)}) collective-permute-start(bf16[128,1152]{1,0:T(8,128)(2,1)S(1)} %get-tuple-element.31), channel_id=1, source_target_pairs={{0,1},{1,0},{2,3},{3,2},{4,5},{5,4},{6,7},{7,6},{8,9},{9,8},{10,11... | collective-permute-start | bytes 884744 | tf_op jit(solution)/shard_map/ppermute | solution.py:211
  24.6 1.5 %collective-permute-done.2.recv_ref = bf16[128,1152]{1,0:T(8,128)(2,1)S(1)} collective-permute-done((bf16[128,1152]{1,0:T(8,128)(2,1)S(1)}, bf16[128,1152]{1,0:T(8,128)(2,1)S(1)}, u32[]{:S(2)}, u32[]{:S(2)}) %collective-permute-start.2) | collective-permute-done | bytes 294944 | tf_op jit(solution)/shard_map/ppermute | solution.py:211
  26.2 0.3 scatter.1
  26.4 0.0 copy-start.1
  26.4 2.6 %collective-permute-start.4 = (bf16[32,1152]{1,0:T(8,128)(2,1)S(1)}, bf16[32,1152]{1,0:T(8,128)(2,1)S(1)}, u32[]{:S(2)}, u32[]{:S(2)}) collective-permute-start(bf16[32,1152]{1,0:T(8,128)(2,1)S(1)} %get-tuple-element.34), channel_id=1, source_target_pairs={{0,2},{1,3},{2,0},{3,1},{4,6},{5,7},{6,4},{7,5},{8,10},{9,11},{10,... | collective-permute-start | bytes 221192 | tf_op jit(solution)/shard_map/ppermute | solution.py:211
  29.1 4.3 %collective-permute-start.5 = (bf16[32,1152]{1,0:T(8,128)(2,1)S(1)}, bf16[32,1152]{1,0:T(8,128)(2,1)S(1)}, u32[]{:S(2)}, u32[]{:S(2)}) collective-permute-start(bf16[32,1152]{1,0:T(8,128)(2,1)S(1)} %get-tuple-element.35), channel_id=1, source_target_pairs={{0,4},{1,5},{2,6},{3,7},{4,0},{5,1},{6,2},{7,3},{8,12},{9,13},{10,... | collective-permute-start | bytes 221192 | tf_op jit(solution)/shard_map/ppermute | solution.py:211
  33.4 2.5 %collective-permute-start.6 = (bf16[32,1152]{1,0:T(8,128)(2,1)S(1)}, bf16[32,1152]{1,0:T(8,128)(2,1)S(1)}, u32[]{:S(2)}, u32[]{:S(2)}) collective-permute-start(bf16[32,1152]{1,0:T(8,128)(2,1)S(1)} %get-tuple-element.36), channel_id=1, source_target_pairs={{0,6},{1,7},{2,4},{3,5},{4,2},{5,3},{6,0},{7,1},{8,14},{9,15},{10,... | collective-permute-start | bytes 221192 | tf_op jit(solution)/shard_map/ppermute | solution.py:211
  35.8 0.7 collective-permute-done.4.one_ref
  36.5 1.3 %collective-permute-done.5.two_ref = bf16[32,1152]{1,0:T(8,128)(2,1)S(1)} collective-permute-done((bf16[32,1152]{1,0:T(8,128)(2,1)S(1)}, bf16[32,1152]{1,0:T(8,128)(2,1)S(1)}, u32[]{:S(2)}, u32[]{:S(2)}) %collective-permute-start.5) | collective-permute-done | bytes 73760 | tf_op jit(solution)/shard_map/ppermute | solution.py:211
  37.8 2.6 %collective-permute-done.6.three_ref = bf16[32,1152]{1,0:T(8,128)(2,1)S(1)} collective-permute-done((bf16[32,1152]{1,0:T(8,128)(2,1)S(1)}, bf16[32,1152]{1,0:T(8,128)(2,1)S(1)}, u32[]{:S(2)}, u32[]{:S(2)}) %collective-permute-start.6) | collective-permute-done | bytes 73760 | tf_op jit(solution)/shard_map/ppermute | solution.py:211
  40.4 0.2 sum.1
  40.6 0.0 collective-permute-done.8
  40.6 9.9 %collective-permute-start.10 = (bf16[1,224,896]{2,1,0:T(8,128)(2,1)S(1)}, bf16[1,224,896]{2,1,0:T(8,128)(2,1)S(1)}, u32[]{:S(2)}, u32[]{:S(2)}) collective-permute-start(bf16[1,224,896]{2,1,0:T(8,128)(2,1)S(1)} %collective-permute-done.7), channel_id=1, source_target_pairs={{0,248},{8,240},{16,232},{24,224},{32,216},{40,208},{48,200},{56,1... | collective-permute-start | bytes 1204232 | tf_op jit(solution)/shard_map/ppermute | solution.py:219
  50.5 4.7 %collective-permute-start.17 = (bf16[1,224,896]{2,1,0:T(8,128)(2,1)S(1)}, bf16[1,224,896]{2,1,0:T(8,128)(2,1)S(1)}, u32[]{:S(2)}, u32[]{:S(2)}) collective-permute-start(bf16[1,224,896]{2,1,0:T(8,128)(2,1)S(1)} %copy-done.8), channel_id=1, source_target_pairs={{248,504},{504,248},{249,505},{505,249},{250,506},{506,250},{251,5... | collective-permute-start | bytes 1204232 | tf_op jit(solution)/shard_map/ppermute | solution.py:230
  55.3 0.7 collective-permute-start.14
  56.0 4.5 %collective-permute-start.9 = (bf16[32,896]{1,0:T(8,128)(2,1)S(1)}, bf16[32,896]{1,0:T(8,128)(2,1)S(1)}, u32[]{:S(2)}, u32[]{:S(2)}) collective-permute-start(bf16[32,896]{1,0:T(8,128)(2,1)S(1)} %get-tuple-element.40), channel_id=1, source_target_pairs={{0,504},{8,496},{16,488},{24,480},{32,472},{40,464},{48,456},{56,4... | collective-permute-start | bytes 172040 | tf_op jit(solution)/shard_map/ppermute | solution.py:269
  60.4 12.9 %collective-permute-done.9.far_ref = bf16[32,896]{1,0:T(8,128)(2,1)S(1)} collective-permute-done((bf16[32,896]{1,0:T(8,128)(2,1)S(1)}, bf16[32,896]{1,0:T(8,128)(2,1)S(1)}, u32[]{:S(2)}, u32[]{:S(2)}) %collective-permute-start.9) | collective-permute-done | bytes 57376 | tf_op jit(solution)/shard_map/ppermute | solution.py:269
  73.3 0.5 step.1.own_ref
  73.9 0.0 copy-start.3
  73.9 0.0 copy-start.10
  73.9 0.0 collective-permute-done.10.xm_ref
  73.9 4.3 %collective-permute-start.13 = (bf16[32,1408]{1,0:T(8,128)(2,1)S(1)}, bf16[32,1408]{1,0:T(8,128)(2,1)S(1)}, u32[]{:S(2)}, u32[]{:S(2)}) collective-permute-start(bf16[32,1408]{1,0:T(8,128)(2,1)S(1)} %step.1.own_ref), channel_id=1, source_target_pairs={{0,6},{1,7},{2,4},{3,5},{4,2},{5,3},{6,0},{7,1},{8,14},{9,15},{10,... | collective-permute-start | bytes 270344 | tf_op jit(solution)/shard_map/ppermute | solution.py:211
  78.2 1.9 %collective-permute-start.12 = (bf16[32,1408]{1,0:T(8,128)(2,1)S(1)}, bf16[32,1408]{1,0:T(8,128)(2,1)S(1)}, u32[]{:S(2)}, u32[]{:S(2)}) collective-permute-start(bf16[32,1408]{1,0:T(8,128)(2,1)S(1)} %step.1.own_ref), channel_id=1, source_target_pairs={{0,4},{1,5},{2,6},{3,7},{4,0},{5,1},{6,2},{7,3},{8,12},{9,13},{10,... | collective-permute-start | bytes 270344 | tf_op jit(solution)/shard_map/ppermute | solution.py:211
  80.1 3.4 %collective-permute-start.11 = (bf16[32,1408]{1,0:T(8,128)(2,1)S(1)}, bf16[32,1408]{1,0:T(8,128)(2,1)S(1)}, u32[]{:S(2)}, u32[]{:S(2)}) collective-permute-start(bf16[32,1408]{1,0:T(8,128)(2,1)S(1)} %step.1.own_ref), channel_id=1, source_target_pairs={{0,2},{1,3},{2,0},{3,1},{4,6},{5,7},{6,4},{7,5},{8,10},{9,11},{10,... | collective-permute-start | bytes 270344 | tf_op jit(solution)/shard_map/ppermute | solution.py:211
  83.5 4.3 %collective-permute-start.16 = (bf16[1,224,896]{2,1,0:T(8,128)(2,1)S(1)}, bf16[1,224,896]{2,1,0:T(8,128)(2,1)S(1)}, u32[]{:S(2)}, u32[]{:S(2)}) collective-permute-start(bf16[1,224,896]{2,1,0:T(8,128)(2,1)S(1)} %collective-permute-done.3), channel_id=1, source_target_pairs={{248,504},{504,248},{249,505},{505,249},{250,506},{506,250},{251,5... | collective-permute-start | bytes 1204232 | tf_op jit(solution)/shard_map/ppermute | solution.py:230
  87.8 2.5 %collective-permute-start.18 = (bf16[1,224,896]{2,1,0:T(8,128)(2,1)S(1)}, bf16[1,224,896]{2,1,0:T(8,128)(2,1)S(1)}, u32[]{:S(2)}, u32[]{:S(2)}) collective-permute-start(bf16[1,224,896]{2,1,0:T(8,128)(2,1)S(1)} %collective-permute-done.17), channel_id=1, source_target_pairs={{248,0},{504,256},{249,1},{505,257},{250,2},{506,258},{251,3},{507... | collective-permute-start | bytes 1204232 | tf_op jit(solution)/shard_map/ppermute | solution.py:274
  90.3 0.0 collective-permute-done.12.two_ref
  90.3 0.0 collective-permute-done.11.one_ref
  90.4 0.0 collective-permute-done.14.cm_ref
  90.4 1.9 %collective-permute-start.15 = (bf16[128,1408]{1,0:T(8,128)(2,1)S(1)}, bf16[128,1408]{1,0:T(8,128)(2,1)S(1)}, u32[]{:S(2)}, u32[]{:S(2)}) collective-permute-start(bf16[128,1408]{1,0:T(8,128)(2,1)S(1)} %gather.1.mine_ref), channel_id=1, source_target_pairs={{0,1},{1,0},{2,3},{3,2},{4,5},{5,4},{6,7},{7,6},{8,9},{9,8},{10,11... | collective-permute-start | bytes 1081352 | tf_op jit(solution)/shard_map/ppermute | solution.py:211
  92.3 15.3 %collective-permute-done.16.far_a_ref = bf16[1,224,896]{2,1,0:T(8,128)(2,1)S(1)} collective-permute-done((bf16[1,224,896]{2,1,0:T(8,128)(2,1)S(1)}, bf16[1,224,896]{2,1,0:T(8,128)(2,1)S(1)}, u32[]{:S(2)}, u32[]{:S(2)}) %collective-permute-start.16) | collective-permute-done | bytes 401440 | tf_op jit(solution)/shard_map/ppermute | solution.py:230
  107.6 0.0 collective-permute-done.18.far_b_ref
  107.7 2.3 %finish.1 = (bf16[1,224,896]{2,1,0:T(8,128)(2,1)}, bf16[1,224,896]{2,1,0:T(8,128)(2,1)}, bf16[1,256,896]{2,1,0:T(8,128)(2,1)}, bf16[1,256,896]{2,1,0:T(8,128)(2,1)}) custom-call(bf16[128,1408]{1,0:T(8,128)(2,1)S(1)} %gather.1.mine_ref, bf16[128,1408]{1,0:T(8,128)(2,1)S(1)} %collective-permute-done.15.other_ref, ...), custom_call_target="tpu_custom_call" | custom-call | flops 616562688 | bytes 4194304 | tf_op jit(solution)/shard_map/finish/pallas_call | solution.py:284
  (21 shorter events, 0.1 us)
Async XLA Ops:
  0.6 20.6 %collective-permute-start = (bf16[1,224,896]{2,1,0:T(8,128)(2,1)}, bf16[1,224,896]{2,1,0:T(8,128)(2,1)S(1)}, u32[]{:S(2)}, u32[]{:S(2)}) collective-permute-start(bf16[1,224,896]{2,1,0:T(8,128)(2,1)} %sa_ref.1), channel_id=1, source_target_pairs={{8,0},{16,8},{24,16},{32,24},{40,32},{48,40},{56,48},{64,56},{72,6... | collective-permute-start | bytes 1204232 | tf_op jit(solution)/shard_map/ppermute | solution.py:232
  3.9 18.2 %collective-permute-start.1 = (bf16[1,224,896]{2,1,0:T(8,128)(2,1)}, bf16[1,224,896]{2,1,0:T(8,128)(2,1)S(1)}, u32[]{:S(2)}, u32[]{:S(2)}) collective-permute-start(bf16[1,224,896]{2,1,0:T(8,128)(2,1)} %sb_ref.1), channel_id=1, source_target_pairs={{0,8},{8,16},{16,24},{24,32},{32,40},{40,48},{48,56},{56,64},{64,7... | collective-permute-start | bytes 1204232 | tf_op jit(solution)/shard_map/ppermute | solution.py:228
  5.2 19.4 %collective-permute-start.3 = (bf16[1,224,896]{2,1,0:T(8,128)(2,1)}, bf16[1,224,896]{2,1,0:T(8,128)(2,1)S(1)}, u32[]{:S(2)}, u32[]{:S(2)}) collective-permute-start(bf16[1,224,896]{2,1,0:T(8,128)(2,1)} %sa_ref.1), channel_id=1, source_target_pairs={{0,248},{256,504},{1,249},{257,505},{2,250},{258,506},{3,251},{259... | collective-permute-start | bytes 1204232 | tf_op jit(solution)/shard_map/ppermute | solution.py:235
  6.5 34.1 %collective-permute-start.7 = (bf16[1,224,896]{2,1,0:T(8,128)(2,1)}, bf16[1,224,896]{2,1,0:T(8,128)(2,1)S(1)}, u32[]{:S(2)}, u32[]{:S(2)}) collective-permute-start(bf16[1,224,896]{2,1,0:T(8,128)(2,1)} %xb_ref.3), channel_id=1, source_target_pairs={{0,256},{8,264},{16,272},{24,280},{32,288},{40,296},{48,304},{56,3... | collective-permute-start | bytes 1204232 | tf_op jit(solution)/shard_map/ppermute | solution.py:216
  16.5 1.2 %copy-start = (bf16[1,2,256,896]{3,2,1,0:T(8,128)(2,1)S(1)}, bf16[1,2,256,896]{3,2,1,0:T(8,128)(2,1)}, u32[]{:S(2)}) copy-start(bf16[1,2,256,896]{3,2,1,0:T(8,128)(2,1)} %wc_ref.3) | copy-start | bytes 2752516
  17.7 1.0 copy-start.2
  18.7 1.0 copy-start.4
  19.7 0.7 copy-start.9
  20.4 1.0 copy-start.8
  20.4 1.7 %copy-start.6 = (bf16[1,2,256,896]{3,2,1,0:T(8,128)(2,1)S(1)}, bf16[1,2,256,896]{3,2,1,0:T(8,128)(2,1)}, u32[]{:S(2)}) copy-start(bf16[1,2,256,896]{3,2,1,0:T(8,128)(2,1)} %we_ref.1) | copy-start | bytes 2752516
  20.4 1.7 %copy-start.7 = (bf16[1,224,896]{2,1,0:T(8,128)(2,1)S(1)}, bf16[1,224,896]{2,1,0:T(8,128)(2,1)}, u32[]{:S(2)}) copy-start(bf16[1,224,896]{2,1,0:T(8,128)(2,1)} %sa_ref.1) | copy-start | bytes 1204228
  21.4 19.2 %collective-permute-start.8 = (bf16[1,224,896]{2,1,0:T(8,128)(2,1)S(1)}, bf16[1,224,896]{2,1,0:T(8,128)(2,1)S(1)}, u32[]{:S(2)}, u32[]{:S(2)}) collective-permute-start(bf16[1,224,896]{2,1,0:T(8,128)(2,1)S(1)} %copy-done.8), channel_id=1, source_target_pairs={{0,240},{8,232},{16,224},{24,216},{32,208},{40,200},{48,192},{56,1... | collective-permute-start | bytes 1204232 | tf_op jit(solution)/shard_map/ppermute | solution.py:226
  22.7 3.5 %collective-permute-start.2 = (bf16[128,1152]{1,0:T(8,128)(2,1)S(1)}, bf16[128,1152]{1,0:T(8,128)(2,1)S(1)}, u32[]{:S(2)}, u32[]{:S(2)}) collective-permute-start(bf16[128,1152]{1,0:T(8,128)(2,1)S(1)} %get-tuple-element.31), channel_id=1, source_target_pairs={{0,1},{1,0},{2,3},{3,2},{4,5},{5,4},{6,7},{7,6},{8,9},{9,8},{10,11... | collective-permute-start | bytes 884744 | tf_op jit(solution)/shard_map/ppermute | solution.py:211
  26.2 47.2 %copy-start.11 = (f32[1,2,256]{2,1,0:T(2,128)S(1)}, f32[1,2,256]{2,1,0:T(2,128)}, u32[]{:S(2)}) copy-start(f32[1,2,256]{2,1,0:T(2,128)} %gain_ref.4) | copy-start | bytes 6148
  26.2 81.5 %copy-start.5 = (bf16[1,224,896]{2,1,0:T(8,128)(2,1)S(1)}, bf16[1,224,896]{2,1,0:T(8,128)(2,1)}, u32[]{:S(2)}) copy-start(bf16[1,224,896]{2,1,0:T(8,128)(2,1)} %xb_ref.3) | copy-start | bytes 1204228
  26.4 81.2 %copy-start.1 = (bf16[1,2,256,896]{3,2,1,0:T(8,128)(2,1)S(1)}, bf16[1,2,256,896]{3,2,1,0:T(8,128)(2,1)}, u32[]{:S(2)}) copy-start(bf16[1,2,256,896]{3,2,1,0:T(8,128)(2,1)} %wc_ref.3) | copy-start | bytes 2752516
  26.4 10.1 %collective-permute-start.4 = (bf16[32,1152]{1,0:T(8,128)(2,1)S(1)}, bf16[32,1152]{1,0:T(8,128)(2,1)S(1)}, u32[]{:S(2)}, u32[]{:S(2)}) collective-permute-start(bf16[32,1152]{1,0:T(8,128)(2,1)S(1)} %get-tuple-element.34), channel_id=1, source_target_pairs={{0,2},{1,3},{2,0},{3,1},{4,6},{5,7},{6,4},{7,5},{8,10},{9,11},{10,... | collective-permute-start | bytes 221192 | tf_op jit(solution)/shard_map/ppermute | solution.py:211
  29.1 8.8 %collective-permute-start.5 = (bf16[32,1152]{1,0:T(8,128)(2,1)S(1)}, bf16[32,1152]{1,0:T(8,128)(2,1)S(1)}, u32[]{:S(2)}, u32[]{:S(2)}) collective-permute-start(bf16[32,1152]{1,0:T(8,128)(2,1)S(1)} %get-tuple-element.35), channel_id=1, source_target_pairs={{0,4},{1,5},{2,6},{3,7},{4,0},{5,1},{6,2},{7,3},{8,12},{9,13},{10,... | collective-permute-start | bytes 221192 | tf_op jit(solution)/shard_map/ppermute | solution.py:211
  33.4 7.1 %collective-permute-start.6 = (bf16[32,1152]{1,0:T(8,128)(2,1)S(1)}, bf16[32,1152]{1,0:T(8,128)(2,1)S(1)}, u32[]{:S(2)}, u32[]{:S(2)}) collective-permute-start(bf16[32,1152]{1,0:T(8,128)(2,1)S(1)} %get-tuple-element.36), channel_id=1, source_target_pairs={{0,6},{1,7},{2,4},{3,5},{4,2},{5,3},{6,0},{7,1},{8,14},{9,15},{10,... | collective-permute-start | bytes 221192 | tf_op jit(solution)/shard_map/ppermute | solution.py:211
  40.6 33.3 %collective-permute-start.10 = (bf16[1,224,896]{2,1,0:T(8,128)(2,1)S(1)}, bf16[1,224,896]{2,1,0:T(8,128)(2,1)S(1)}, u32[]{:S(2)}, u32[]{:S(2)}) collective-permute-start(bf16[1,224,896]{2,1,0:T(8,128)(2,1)S(1)} %collective-permute-done.7), channel_id=1, source_target_pairs={{0,248},{8,240},{16,232},{24,224},{32,216},{40,208},{48,200},{56,1... | collective-permute-start | bytes 1204232 | tf_op jit(solution)/shard_map/ppermute | solution.py:219
  50.5 32.9 %collective-permute-start.17 = (bf16[1,224,896]{2,1,0:T(8,128)(2,1)S(1)}, bf16[1,224,896]{2,1,0:T(8,128)(2,1)S(1)}, u32[]{:S(2)}, u32[]{:S(2)}) collective-permute-start(bf16[1,224,896]{2,1,0:T(8,128)(2,1)S(1)} %copy-done.8), channel_id=1, source_target_pairs={{248,504},{504,248},{249,505},{505,249},{250,506},{506,250},{251,5... | collective-permute-start | bytes 1204232 | tf_op jit(solution)/shard_map/ppermute | solution.py:230
  55.3 35.1 %collective-permute-start.14 = (bf16[1,224,896]{2,1,0:T(8,128)(2,1)S(1)}, bf16[1,224,896]{2,1,0:T(8,128)(2,1)S(1)}, u32[]{:S(2)}, u32[]{:S(2)}) collective-permute-start(bf16[1,224,896]{2,1,0:T(8,128)(2,1)S(1)} %collective-permute-done.8), channel_id=1, source_target_pairs={{0,256},{8,264},{16,272},{24,280},{32,288},{40,296},{48,304},{56,3... | collective-permute-start | bytes 1204232 | tf_op jit(solution)/shard_map/ppermute | solution.py:222
  56.0 17.4 %collective-permute-start.9 = (bf16[32,896]{1,0:T(8,128)(2,1)S(1)}, bf16[32,896]{1,0:T(8,128)(2,1)S(1)}, u32[]{:S(2)}, u32[]{:S(2)}) collective-permute-start(bf16[32,896]{1,0:T(8,128)(2,1)S(1)} %get-tuple-element.40), channel_id=1, source_target_pairs={{0,504},{8,496},{16,488},{24,480},{32,472},{40,464},{48,456},{56,4... | collective-permute-start | bytes 172040 | tf_op jit(solution)/shard_map/ppermute | solution.py:269
  73.9 33.8 %copy-start.3 = (bf16[1,224,896]{2,1,0:T(8,128)(2,1)S(1)}, bf16[1,224,896]{2,1,0:T(8,128)(2,1)}, u32[]{:S(2)}) copy-start(bf16[1,224,896]{2,1,0:T(8,128)(2,1)} %xa_ref.3) | copy-start | bytes 1204228
  73.9 33.8 %copy-start.10 = (f32[1,2,896]{2,1,0:T(2,128)S(1)}, f32[1,2,896]{2,1,0:T(2,128)}, u32[]{:S(2)}) copy-start(f32[1,2,896]{2,1,0:T(2,128)} %gain_ref.5) | copy-start | bytes 21508
  73.9 13.9 %collective-permute-start.13 = (bf16[32,1408]{1,0:T(8,128)(2,1)S(1)}, bf16[32,1408]{1,0:T(8,128)(2,1)S(1)}, u32[]{:S(2)}, u32[]{:S(2)}) collective-permute-start(bf16[32,1408]{1,0:T(8,128)(2,1)S(1)} %step.1.own_ref), channel_id=1, source_target_pairs={{0,6},{1,7},{2,4},{3,5},{4,2},{5,3},{6,0},{7,1},{8,14},{9,15},{10,... | collective-permute-start | bytes 270344 | tf_op jit(solution)/shard_map/ppermute | solution.py:211
  78.2 12.2 %collective-permute-start.12 = (bf16[32,1408]{1,0:T(8,128)(2,1)S(1)}, bf16[32,1408]{1,0:T(8,128)(2,1)S(1)}, u32[]{:S(2)}, u32[]{:S(2)}) collective-permute-start(bf16[32,1408]{1,0:T(8,128)(2,1)S(1)} %step.1.own_ref), channel_id=1, source_target_pairs={{0,4},{1,5},{2,6},{3,7},{4,0},{5,1},{6,2},{7,3},{8,12},{9,13},{10,... | collective-permute-start | bytes 270344 | tf_op jit(solution)/shard_map/ppermute | solution.py:211
  80.1 10.2 %collective-permute-start.11 = (bf16[32,1408]{1,0:T(8,128)(2,1)S(1)}, bf16[32,1408]{1,0:T(8,128)(2,1)S(1)}, u32[]{:S(2)}, u32[]{:S(2)}) collective-permute-start(bf16[32,1408]{1,0:T(8,128)(2,1)S(1)} %step.1.own_ref), channel_id=1, source_target_pairs={{0,2},{1,3},{2,0},{3,1},{4,6},{5,7},{6,4},{7,5},{8,10},{9,11},{10,... | collective-permute-start | bytes 270344 | tf_op jit(solution)/shard_map/ppermute | solution.py:211
  83.5 24.1 %collective-permute-start.16 = (bf16[1,224,896]{2,1,0:T(8,128)(2,1)S(1)}, bf16[1,224,896]{2,1,0:T(8,128)(2,1)S(1)}, u32[]{:S(2)}, u32[]{:S(2)}) collective-permute-start(bf16[1,224,896]{2,1,0:T(8,128)(2,1)S(1)} %collective-permute-done.3), channel_id=1, source_target_pairs={{248,504},{504,248},{249,505},{505,249},{250,506},{506,250},{251,5... | collective-permute-start | bytes 1204232 | tf_op jit(solution)/shard_map/ppermute | solution.py:230
  87.8 19.8 %collective-permute-start.18 = (bf16[1,224,896]{2,1,0:T(8,128)(2,1)S(1)}, bf16[1,224,896]{2,1,0:T(8,128)(2,1)S(1)}, u32[]{:S(2)}, u32[]{:S(2)}) collective-permute-start(bf16[1,224,896]{2,1,0:T(8,128)(2,1)S(1)} %collective-permute-done.17), channel_id=1, source_target_pairs={{248,0},{504,256},{249,1},{505,257},{250,2},{506,258},{251,3},{507... | collective-permute-start | bytes 1204232 | tf_op jit(solution)/shard_map/ppermute | solution.py:274
  90.4 17.2 %collective-permute-start.15 = (bf16[128,1408]{1,0:T(8,128)(2,1)S(1)}, bf16[128,1408]{1,0:T(8,128)(2,1)S(1)}, u32[]{:S(2)}, u32[]{:S(2)}) collective-permute-start(bf16[128,1408]{1,0:T(8,128)(2,1)S(1)} %gather.1.mine_ref), channel_id=1, source_target_pairs={{0,1},{1,0},{2,3},{3,2},{4,5},{5,4},{6,7},{7,6},{8,9},{9,8},{10,11... | collective-permute-start | bytes 1081352 | tf_op jit(solution)/shard_map/ppermute | solution.py:211
